TPU v7x, 1024 devices: a whole 8x8x8 slice. The times are simulated.
1024 devices in a mesh: fsdp: 128 (over y, z, core), own: 8 (over x).
Axes of the slice: x: 8, y: 8, z: 8, core: 2. Of those that a mesh axis runs over, the one named last changes fastest.
Arguments:
- gradient: bfloat16 [128, 256, 256], P(None, 'fsdp'), may hold values from -6 to 6
- refresh: int32 [128, 2], P('fsdp'), may hold values 0 or 1
- left_stat: float32 [128, 256, 256], P('fsdp'), as said below
- right_stat: float32 [128, 256, 256], P('fsdp'), as said below
- left_root: bfloat16 [128, 256, 256], P('fsdp'), as said below
- right_root: bfloat16 [128, 256, 256], P('fsdp'), as said below
Outputs:
- grafted: bfloat16 [128, 256, 256], P(None, 'fsdp')
- new_left: float32 [128, 256, 256], P('fsdp')
- new_right: float32 [128, 256, 256], P('fsdp')
- new_left_root: bfloat16 [128, 256, 256], P('fsdp')
- new_right_root: bfloat16 [128, 256, 256], P('fsdp')
Inputs may be any that keep to these rules, and one draw needn't show every extreme that they name: `left_stat`: each block is symmetric positive definite. `right_stat`: each block is symmetric positive definite. `left_root`: each block is symmetric. `right_root`: each block is symmetric.
All inputs are finite; a program needn't handle non-finite values. No bound on the sum of `refresh` on one device may be relied on, other than what follows from the above.
Results may differ from a plain program's by a relative error of at most 0.0053.
Values may be sent and summed in bfloat16 or wider, within the bound.
A program may use at most 32 MiB of HBM per device.

v0:
```python
import jax
import jax.numpy as jnp
from jax import lax
from jax.sharding import PartitionSpec as P

ITERS = 5


decay_rate = 0.8
epsilon = 1e-06


def from_root(value, axis, root):
    mine = lax.axis_index(axis) == root
    return lax.psum(jnp.where(mine, value, jnp.zeros_like(value)), axis)


def inverse_fourth_root(stat):
    identity = jnp.eye(stat.shape[0], dtype=jnp.float32)
    frobenius = jnp.sqrt(jnp.sum(stat * stat))
    matrix = stat / frobenius
    root_matrix = identity * frobenius ** (-0.25)
    for sweep in range(ITERS):
        factor = (5.0 * identity - matrix) * 0.25
        root_matrix = jnp.dot(root_matrix, factor, precision=lax.Precision.HIGHEST)
        square = jnp.dot(factor, factor, precision=lax.Precision.HIGHEST)
        fourth = jnp.dot(square, square, precision=lax.Precision.HIGHEST)
        matrix = jnp.dot(fourth, matrix, precision=lax.Precision.HIGHEST)
    return root_matrix


def maybe_refresh(wanted, stat, previous):
    return lax.cond(
        wanted, lambda: inverse_fourth_root(stat).astype(jnp.bfloat16), lambda: previous
    )


def shards(gradient, refresh, left_stat, right_stat, left_root, right_root):
    whole_block = lax.all_to_all(gradient, "fsdp", split_axis=0, concat_axis=1, tiled=True)[0]
    left_gram = lax.dot_general(
        whole_block, whole_block, (((1,), (1,)), ((), ())), preferred_element_type=jnp.float32
    )
    right_gram = lax.dot_general(
        whole_block, whole_block, (((0,), (0,)), ((), ())), preferred_element_type=jnp.float32
    )
    new_left = decay_rate * left_stat[0] + (1.0 - decay_rate) * left_gram
    new_right = decay_rate * right_stat[0] + (1.0 - decay_rate) * right_gram
    replicas = lax.axis_size("own")
    owner_index = lax.axis_index("fsdp") % replicas
    own_index = lax.axis_index("own")
    left_wanted = (refresh[0, 0] == 1) & (own_index == owner_index)
    left_new = maybe_refresh(left_wanted, new_left, left_root[0])
    right_wanted = (refresh[0, 1] == 1) & (own_index == owner_index)
    right_new = maybe_refresh(right_wanted, new_right, right_root[0])
    left_new, right_new = (
        from_root(left_new, "own", owner_index),
        from_root(right_new, "own", owner_index),
    )
    half_product = jnp.dot(left_new, whole_block, preferred_element_type=jnp.float32).astype(
        jnp.bfloat16
    )
    preconditioned = jnp.dot(half_product, right_new, preferred_element_type=jnp.float32)
    wide_block = whole_block.astype(jnp.float32)
    grad_norm = jnp.sqrt(jnp.sum(wide_block * wide_block))
    grafted = (
        preconditioned * (grad_norm / jnp.sqrt(jnp.sum(preconditioned * preconditioned) + epsilon))
    ).astype(jnp.bfloat16)
    row_shards = lax.all_to_all(grafted[None], "fsdp", split_axis=1, concat_axis=0, tiled=True)
    return (row_shards, new_left[None], new_right[None], left_new[None], right_new[None])


def solution(mesh):
    placed = (
        P(None, "fsdp", None),
        P("fsdp", None),
        P("fsdp", None, None),
        P("fsdp", None, None),
        P("fsdp", None, None),
        P("fsdp", None, None),
    )
    return jax.shard_map(
        shards,
        mesh=mesh,
        in_specs=placed,
        out_specs=(
            P(None, "fsdp", None),
            P("fsdp", None, None),
            P("fsdp", None, None),
            P("fsdp", None, None),
            P("fsdp", None, None),
        ),
        check_vma=False,
    )
```

profile of v0, /device:TPU:1, one launch (start us, length us, event | category | flops | bytes accessed | tf_op | source)
XLA Modules:
  0.0 185.4 jit_solution(17053603505443424235)
XLA Ops:
  7.2 0.0 copy-start.5
  7.2 25.4 %all-to-all-start = ((bf16[128,2,256]{2,1,0:T(2,128)(2,1)}), bf16[128,2,256]{2,1,0:T(2,128)(2,1)S(1)}, u32[]{:S(2)}, u32[]{:S(2)}) async-start(bf16[128,2,256]{2,1,0:T(2,128)(2,1)} %param.10), calls=%async_computation | async-start | bytes 262144 | tf_op jit(solution)/shard_map/all_to_all | solution.py:39
  32.6 0.0 all-reduce.3.cloned.1.call-start
  32.6 0.0 copy-start.7
  32.6 0.6 copy-done.7
  33.3 0.6 fusion.150
  35.2 9.6 %all-to-all-done = bf16[128,2,256]{2,1,0:T(2,128)(2,1)S(1)} async-done(((bf16[128,2,256]{2,1,0:T(2,128)(2,1)}), bf16[128,2,256]{2,1,0:T(2,128)(2,1)S(1)}, u32[]{:S(2)}, u32[]{:S(2)}) %all-to-all-start) | async-done | bytes 131104 | tf_op jit(solution)/shard_map/all_to_all | solution.py:39
  44.8 0.1 squeeze.19
  44.8 0.0 copy-done.5
  44.8 0.0 copy-start.2
  44.9 0.0 copy-start.6
  44.9 0.2 fusion.144
  45.1 0.7 copy-done.2
  45.7 0.1 copy-done.6
  45.9 0.0 copy-start
  45.9 0.9 fusion.146
  46.8 0.0 copy-start.1
  46.8 0.9 copy-done.1
  47.7 0.0 copy-done
  47.7 0.7 broadcast_select_fusion
  48.4 0.0 all-reduce.3.cloned.1.call-update
  48.5 0.9 multiply_reduce_fusion.3
  50.0 87.9 %all-reduce.3.cloned.1.call-done = (bf16[256,256]{1,0:T(8,128)(2,1)}, bf16[256,256]{1,0:T(8,128)(2,1)}) async-done(((bf16[256,256]{1,0:T(8,128)(2,1)}, bf16[256,256]{1,0:T(8,128)(2,1)}), (bf16[256,256]{1,0:T(8,128)(2,1)}, bf16[256,256]{1,0:T(8,128)(2,1)})) %all-reduce.3.cloned.1.call-update) | async-done | bytes 262160 | tf_op jit(solution)/shard_map/psum | solution.py:15
  138.0 1.9 %multiply_reduce_fusion.2 = (f32[]{:T(128)}, f32[256,256]{1,0:T(8,128)S(1)}) fusion(bf16[256,256]{1,0:T(8,128)(2,1)} %get-tuple-element.23, bf16[256,256]{1,0:T(8,128)(2,1)} %get-tuple-element.24, bf16[256,256]{1,0:T(8,128)(2,1)S(1)} %squeeze.19), kind=kOutput, calls=%fused_computation.154 | convolution fusion | flops 67305472 | bytes 655364 | tf_op jit(solution)/shard_map/dot_general | solution.py:62
  140.6 0.2 copy.28
  140.8 0.5 broadcast.245
  141.3 1.4 reduce.3
  142.7 0.1 reshape.27
  142.8 32.4 %all_to_all.21 = bf16[128,2,256]{2,1,0:T(2,128)(2,1)S(1)} all-to-all(bf16[128,2,256]{2,1,0:T(2,128)(2,1)S(1)} %reshape.27), channel_id=1, replica_groups=mesh['fsdp'=128,'own'=8] {'fsdp'}, dimensions={0} | all-to-all | bytes 262144 | tf_op jit(solution)/shard_map/all_to_all | solution.py:68
  175.1 0.1 reshape.28
  175.2 0.7 bitcast_reduce_fusion
  176.0 0.0 copy-start.4
  176.0 0.7 all_to_all.8
  176.7 0.2 copy-done.4
  176.9 0.0 copy-start.3
  176.9 0.7 copy.42
  177.6 0.3 copy-done.3
  177.9 0.7 copy.43
  (3 shorter events, 0.0 us)
Async XLA Ops:
  7.2 37.7 %copy-start.5 = (f32[1,256,256]{2,1,0:T(8,128)S(1)}, f32[1,256,256]{2,1,0:T(8,128)}, u32[]{:S(2)}) copy-start(f32[1,256,256]{2,1,0:T(8,128)} %param.12) | copy-start | bytes 786436
  7.2 37.6 %all-to-all-start = ((bf16[128,2,256]{2,1,0:T(2,128)(2,1)}), bf16[128,2,256]{2,1,0:T(2,128)(2,1)S(1)}, u32[]{:S(2)}, u32[]{:S(2)}) async-start(bf16[128,2,256]{2,1,0:T(2,128)(2,1)} %param.10), calls=%async_computation | async-start | bytes 262144 | tf_op jit(solution)/shard_map/all_to_all | solution.py:39
  32.6 105.4 %all-reduce.3.cloned.1.call-start = ((), (), s32[]{:S(2)}) async-start(), calls=%async_computation.2 | async-start | bytes 524288 | tf_op jit(solution)/shard_map/psum | solution.py:15
  32.6 0.7 copy-start.7
  44.8 0.9 copy-start.2
  44.9 1.0 copy-start.6
  45.9 1.8 copy-start
  46.8 0.9 copy-start.1
  176.0 0.9 copy-start.4
  176.9 1.0 copy-start.3
Sparse Core Ops, SparseCore 0:
  48.6 89.3 all-reduce.2
where the time goes:
time: 185 us
  waiting for transfers between devices  97.5 us (53%)
  blocking collectives  32.4 us (18%)
  starting transfers between devices  25.4 us (14%)
  between operations  16.9 us (9%)
  local copies, waits for them, and re-layouts  7.09 us (4%)
  matrix products  3.07 us (2%)
  other arithmetic  3.01 us (2%)
    psum x1, waiting for transfers between devices, from_root(): return lax.psum(jnp.where(mine, value, jnp.zeros_like(value)), axis)  87.9 us
    all_to_all x1, blocking collectives, shards(): lax.all_to_all(grafted[None], 'fsdp', split_axis=1, concat_axis=0, tiled=...  32.4 us
    all_to_all x1, starting transfers between devices, shards(): lax.all_to_all(gradient, 'fsdp', split_axis=0, concat_axis=1, tiled=True)[0]  25.4 us
    all_to_all x1, waiting for transfers between devices, shards(): lax.all_to_all(gradient, 'fsdp', split_axis=0, concat_axis=1, tiled=True)[0]  9.59 us
    unnamed x21, local copies, waits for them, and re-layouts  4.8 us
  transfers between devices with their start and end apart: 2, of which 2 were waited for; matrix products, arithmetic and copies ran while one was open for 1% of the time, Pallas kernels for 0%

commit v1 on v0

v1 whole, which is shorter than its diff:
```python
import jax
import jax.numpy as jnp
from jax import lax
from jax.experimental import pallas as pl
from jax.experimental.pallas import tpu as pltpu
from jax.sharding import PartitionSpec as P

ITERS = 5
B = 256
Y, Z, C = 8, 8, 2

decay_rate = 0.8
epsilon = 1e-06

f32, bf16 = jnp.float32, jnp.bfloat16
MESH = pl.DeviceIdType.MESH


def dot(a, b, dims=((1,), (0,))):
    return lax.dot_general(a, b, (dims, ((), ())), preferred_element_type=f32)


def split(a):
    high = a.astype(bf16)
    return high, (a - high.astype(f32)).astype(bf16)


def product(a, b):
    return dot(a[0], b[0]) + (dot(a[0], b[1]) + dot(a[1], b[0]))


def inverse_fourth_roots(stats):
    n = range(len(stats))
    rows = lax.broadcasted_iota(jnp.int32, (B, B), 0)
    on_diagonal = rows == lax.broadcasted_iota(jnp.int32, (B, B), 1)
    frobenius = [jnp.sqrt(jnp.sum(s * s, keepdims=True)) for s in stats]
    matrix = [stats[i] / frobenius[i] for i in n]
    root = None
    for sweep in range(ITERS):
        parts = [split(m) for m in matrix]
        if root is None:
            root = [jnp.where(on_diagonal, 1.25, 0.0) - 0.25 * m for m in matrix]
        else:
            root = [1.25 * root[i] - 0.25 * product(split(root[i]), parts[i]) for i in n]
        if sweep < ITERS - 1:
            square = [product(parts[i], parts[i]) for i in n]
            r = [(square[i] - 10.0 * matrix[i]) * 0.0625 for i in n]
            rp = [split(x) for x in r]
            r4 = [3.125 * r[i] + product(rp[i], rp[i]) for i in n]
            matrix = [2.44140625 * matrix[i] + product(split(r4[i]), parts[i]) for i in n]
    scale = [jnp.exp(-0.25 * jnp.log(c)) for c in frobenius]
    return [root[i] * scale[i] for i in n]


def kernel(
    refresh_ref, g_ref, ls_ref, rs_ref, lr_ref, rr_ref,
    out_ref, nl_ref, nr_ref, nlr_ref, nrr_ref,
    relay, block, back, relay_back, ls, rs, lr, rr, nl, nr, nlr, nrr,
    load_sem, store_sem, send1, recv1, send2, recv2, send3, recv3, send4, recv4,
):
    me = lax.axis_index("fsdp")
    own = lax.axis_index("own")
    y, z, c = me // (Z * C), (me // C) % Z, me % C

    def at(py, pz, pc):
        return ((py * Z + pz) * C + pc, own)

    loads = [
        pltpu.make_async_copy(src, dst, load_sem.at[i])
        for i, (src, dst) in enumerate(((ls_ref, ls), (rs_ref, rs), (lr_ref, lr), (rr_ref, rr)))
    ]
    for copy in loads:
        copy.start()

    barrier = pltpu.get_barrier_semaphore()
    partners = 0
    for i in range(Y):
        for pc in range(C):
            if i:
                pl.semaphore_signal(barrier, inc=1, device_id=at((y + i) % Y, z, pc), device_id_type=MESH)
                pl.semaphore_signal(barrier, inc=1, device_id=at(y, (z + i) % Z, pc), device_id_type=MESH)
                partners += 2
    pl.semaphore_signal(barrier, inc=1, device_id=at(y, z, 1 - c), device_id_type=MESH)
    partners += 1
    pl.semaphore_wait(barrier, partners)

    def remote(src, dst, send, recv, to):
        return pltpu.make_async_remote_copy(
            src_ref=src, dst_ref=dst, send_sem=send, recv_sem=recv, device_id=to, device_id_type=MESH
        )

    def drained(ref, sem):
        pltpu.make_async_copy(ref, ref, sem).wait()

    for i in range(1, Z):
        pz = (z + i) % Z
        remote(g_ref.at[:, pz, 0], relay.at[:, z, c], send1, recv1, at(y, pz, 0)).start()
        py = (y + i) % Y
        remote(g_ref.at[py, :, 1], relay.at[:, y, c], send1, recv1, at(py, z, 1)).start()

    @pl.when(c == 0)
    def _():
        remote(g_ref.at[y, :, 1], relay.at[:, y, c], send1, recv1, at(y, z, 1)).start()
        pltpu.make_async_copy(g_ref.at[:, z, 0], relay.at[:, z, c], recv1).start()

    @pl.when(c == 1)
    def _():
        remote(g_ref.at[:, z, 0], relay.at[:, z, c], send1, recv1, at(y, z, 0)).start()
        pltpu.make_async_copy(g_ref.at[y, :, 1], relay.at[:, y, c], recv1).start()

    drained(relay, recv1)

    @pl.when(c == 0)
    def _():
        for i in range(1, Y):
            py = (y + i) % Y
            remote(relay.at[py], block.at[y], send2, recv2, at(py, z, 0)).start()
        pltpu.make_async_copy(relay.at[y], block.at[y], recv2).start()

    @pl.when(c == 1)
    def _():
        for i in range(1, Z):
            pz = (z + i) % Z
            remote(relay.at[pz], block.at[:, z], send2, recv2, at(y, pz, 1)).start()
        pltpu.make_async_copy(relay.at[z], block.at[:, z], recv2).start()

    drained(relay.at[:, 0:7], send1)
    drained(relay.at[:, 7, 0], send1)
    for copy in loads:
        copy.wait()
    drained(block, recv2)
    drained(block.at[0:7], send2)

    g = block[...].reshape(B, B)
    new_left = decay_rate * ls[...] + (1.0 - decay_rate) * dot(g, g, ((1,), (1,)))
    new_right = decay_rate * rs[...] + (1.0 - decay_rate) * dot(g, g, ((0,), (0,)))
    nl[...] = new_left
    nr[...] = new_right
    stores = [
        pltpu.make_async_copy(src, dst, store_sem.at[i])
        for i, (src, dst) in enumerate(((nl, nl_ref), (nr, nr_ref), (nlr, nlr_ref), (nrr, nrr_ref)))
    ]
    stores[0].start()
    stores[1].start()
    left_fresh, right_fresh = inverse_fourth_roots([new_left, new_right])
    left = jnp.where(refresh_ref[0, 0] == 1, left_fresh.astype(bf16), lr[...])
    right = jnp.where(refresh_ref[0, 1] == 1, right_fresh.astype(bf16), rr[...])
    nlr[...] = left
    nrr[...] = right
    stores[2].start()
    stores[3].start()
    preconditioned = dot(dot(left, g).astype(bf16), right)
    wide = g.astype(f32)
    grad_norm = jnp.sqrt(jnp.sum(wide * wide, keepdims=True))
    norm = jnp.sqrt(jnp.sum(preconditioned * preconditioned, keepdims=True) + epsilon)
    grafted = (preconditioned * (grad_norm / norm)).astype(bf16)
    back[...] = grafted.reshape(Y, Z, C, 2, B)

    @pl.when(c == 0)
    def _():
        for i in range(1, Y):
            py = (y + i) % Y
            remote(back.at[py], relay_back.at[y], send3, recv3, at(py, z, 0)).start()
        pltpu.make_async_copy(back.at[y], relay_back.at[y], recv3).start()

    @pl.when(c == 1)
    def _():
        for i in range(1, Z):
            pz = (z + i) % Z
            remote(back.at[:, pz], relay_back.at[z], send3, recv3, at(y, pz, 1)).start()
        pltpu.make_async_copy(back.at[:, z], relay_back.at[z], recv3).start()

    drained(relay_back, recv3)

    @pl.when(c == 0)
    def _():
        for i in range(1, Z):
            for pc in range(C):
                pz = (z + i) % Z
                remote(relay_back.at[:, pz, pc], out_ref.at[:, z, 0], send4, recv4, at(y, pz, pc)).start()
        remote(relay_back.at[:, z, 1], out_ref.at[:, z, 0], send4, recv4, at(y, z, 1)).start()
        pltpu.make_async_copy(relay_back.at[:, z, 0], out_ref.at[:, z, 0], recv4).start()

    @pl.when(c == 1)
    def _():
        for i in range(1, Y):
            for pc in range(C):
                py = (y + i) % Y
                remote(relay_back.at[:, py, pc], out_ref.at[y, :, 1], send4, recv4, at(py, z, pc)).start()
        remote(relay_back.at[:, y, 0], out_ref.at[y, :, 1], send4, recv4, at(y, z, 0)).start()
        pltpu.make_async_copy(relay_back.at[:, y, 1], out_ref.at[y, :, 1], recv4).start()

    drained(relay_back.at[0:7], send3)
    for copy in stores:
        copy.wait()
    drained(relay_back.at[:, 0:7], send4)
    drained(relay_back.at[:, 7, 0], send4)
    drained(out_ref, recv4)


def shards(gradient, refresh, left_stat, right_stat, left_root, right_root):
    anywhere = pl.BlockSpec(memory_space=pl.ANY)
    square = lambda dtype: jax.ShapeDtypeStruct((B, B), dtype)
    rows = (Y, Z, C, 2, B)
    dma = pltpu.SemaphoreType.DMA
    grafted, new_left, new_right, new_left_root, new_right_root = pl.pallas_call(
        kernel,
        out_shape=(jax.ShapeDtypeStruct(rows, bf16), square(f32), square(f32), square(bf16), square(bf16)),
        in_specs=[pl.BlockSpec(memory_space=pltpu.SMEM)] + [anywhere] * 5,
        out_specs=(anywhere,) * 5,
        scratch_shapes=[pltpu.VMEM(rows, bf16)] * 4
        + [pltpu.VMEM((B, B), t) for t in (f32, f32, bf16, bf16, f32, f32, bf16, bf16)]
        + [dma((4,)), dma((4,))]
        + [dma] * 8,
        compiler_params=pltpu.CompilerParams(
            collective_id=0, has_side_effects=True, vmem_limit_bytes=32 * 1024 * 1024
        ),
    )(
        refresh, gradient.reshape(rows), left_stat[0], right_stat[0], left_root[0], right_root[0]
    )
    return (
        grafted.reshape(Y * Z * C, 2, B), new_left[None], new_right[None], new_left_root[None], new_right_root[None]
    )


def solution(mesh):
    rows, blocks = P(None, "fsdp", None), P("fsdp", None, None)
    return jax.shard_map(
        shards,
        mesh=mesh,
        in_specs=(rows, P("fsdp", None), blocks, blocks, blocks, blocks),
        out_specs=(rows, blocks, blocks, blocks, blocks),
        check_vma=False,
    )
```

time: 185 us -> 59.2 us (0.32)
  waiting for transfers between devices: 97.5 us -> 0 us
  Pallas kernels: 0 us -> 49.6 us
  blocking collectives: 32.4 us -> 0 us
  starting transfers between devices: 25.4 us -> 0 us
  between operations: 16.9 us -> 0.66 us
  matrix products: 3.07 us -> 0 us
  other arithmetic: 3.01 us -> 0 us
    psum x1 -> x0, waiting for transfers between devices: 87.9 us -> none  [from_root(): return lax.psum(jnp.where(mine, value, jnp.zeros_like(value)), axis)]
    pallas_call x0 -> x1, Pallas kernels: none -> 49.6 us  [shards(): pl.pallas_call(kernel, out_shape=(jax.ShapeDtypeStruct(rows, bf16), squar...]
    all_to_all x1 -> x0, blocking collectives: 32.4 us -> none  [shards(): lax.all_to_all(grafted[None], 'fsdp', split_axis=1, concat_axis=0, tiled=...]
    all_to_all x1 -> x0, starting transfers between devices: 25.4 us -> none  [shards(): lax.all_to_all(gradient, 'fsdp', split_axis=0, concat_axis=1, tiled=True)[0]]
    all_to_all x1 -> x0, waiting for transfers between devices: 9.59 us -> none  [shards(): lax.all_to_all(gradient, 'fsdp', split_axis=0, concat_axis=1, tiled=True)[0]]
    unnamed x21 -> x17, local copies, waits for them, and re-layouts: 4.8 us -> 8.63 us
    dot_general x3 -> x0, matrix products: 3.07 us -> none  [the longest x1 1.91 us: shards(): jnp.dot(half_product, right_new, preferred_element_type=jnp.float32)]
  transfers between devices with their start and end apart: 2 -> 0, of which waited for: 2 -> 0; matrix products, arithmetic and copies ran while one was open for 1% -> 0% of each run, Pallas kernels for 0% -> 0%
where the time goes in v1:
time: 59.2 us; the launch traced here: 58.9 us
  Pallas kernels  49.6 us (84%)
  local copies, waits for them, and re-layouts  8.63 us (15%)
  between operations  0.66 us (1%)
    pallas_call x1, Pallas kernels, shards(): pl.pallas_call(kernel, out_shape=(jax.ShapeDtypeStruct(rows, bf16), squar...  49.6 us
    unnamed x17, local copies, waits for them, and re-layouts  8.63 us

profile of v1, /device:TPU:1, one launch (start us, length us, event | category | flops | bytes accessed | tf_op | source)
XLA Modules:
  0.0 58.9 jit_solution(7328573549938671760)
XLA Ops:
  0.6 0.0 copy-start.5
  0.6 0.6 %copy-done.5 = s32[1,2]{1,0:T(1,128)S(1)} copy-done((s32[1,2]{1,0:T(1,128)S(1)}, s32[1,2]{1,0:T(1,128)}, u32[]{:S(2)}) %copy-start.5) | copy-done | bytes 32
  1.3 0.0 copy-start
  1.3 0.9 %copy-done = f32[1,256,256]{2,1,0:T(8,128)S(1)} copy-done((f32[1,256,256]{2,1,0:T(8,128)S(1)}, f32[1,256,256]{2,1,0:T(8,128)}, u32[]{:S(2)}) %copy-start) | copy-done | bytes 262168
  2.2 0.0 copy-start.1
  2.2 0.9 %copy-done.1 = f32[1,256,256]{2,1,0:T(8,128)S(1)} copy-done((f32[1,256,256]{2,1,0:T(8,128)S(1)}, f32[1,256,256]{2,1,0:T(8,128)}, u32[]{:S(2)}) %copy-start.1) | copy-done | bytes 262168
  3.2 0.0 copy-start.2
  3.2 0.9 %copy-done.2 = bf16[128,2,256]{2,1,0:T(2,128)(2,1)S(1)} copy-done((bf16[128,2,256]{2,1,0:T(2,128)(2,1)S(1)}, bf16[128,2,256]{2,1,0:T(2,128)(2,1)}, u32[]{:S(2)}) %copy-start.2) | copy-done | bytes 131096
  4.1 0.0 copy-start.3
  4.1 0.9 %copy-done.3 = bf16[1,256,256]{2,1,0:T(8,128)(2,1)S(1)} copy-done((bf16[1,256,256]{2,1,0:T(8,128)(2,1)S(1)}, bf16[1,256,256]{2,1,0:T(8,128)(2,1)}, u32[]{:S(2)}) %copy-start.3) | copy-done | bytes 131096
  5.0 0.0 copy-start.4
  5.0 0.9 %copy-done.4 = bf16[1,256,256]{2,1,0:T(8,128)(2,1)S(1)} copy-done((bf16[1,256,256]{2,1,0:T(8,128)(2,1)S(1)}, bf16[1,256,256]{2,1,0:T(8,128)(2,1)}, u32[]{:S(2)}) %copy-start.4) | copy-done | bytes 131096
  5.9 49.6 %shard_map.101 = (bf16[8,8,2,2,256]{4,3,2,1,0:T(2,128)(2,1)S(1)}, f32[256,256]{1,0:T(8,128)S(1)}, f32[256,256]{1,0:T(8,128)S(1)}, bf16[256,256]{1,0:T(8,128)(2,1)S(1)}, bf16[256,256]{1,0:T(8,128)(2,1)S(1)}) custom-call(s32[1,2]{1,0:T(1,128)S(1)} %copy-done.5, bf16[8,8,2,2,256]{4,3,2,1,0:T(2,128)(2,1)S(1)} %bitcast.14, f32[256,256]{1,0:T(8,128)S(1)} %bitcast.10, ...), custom_call_target="tpu_custom_call" | custom-call | tf_op jit(solution)/shard_map/pallas_call | solution.py:206
  55.6 0.7 %copy.16 = bf16[128,2,256]{2,1,0:T(2,128)(2,1)} copy(bf16[128,2,256]{2,1,0:T(2,128)(2,1)S(1)} %bitcast.19) | data formatting | bytes 262144
  56.2 0.7 %copy.17 = f32[1,256,256]{2,1,0:T(8,128)} copy(f32[1,256,256]{2,1,0:T(8,128)S(1)} %bitcast.13) | data formatting | bytes 524288
  56.9 0.7 %copy.18 = f32[1,256,256]{2,1,0:T(8,128)} copy(f32[1,256,256]{2,1,0:T(8,128)S(1)} %bitcast.12) | data formatting | bytes 524288
  57.6 0.7 %copy.19 = bf16[1,256,256]{2,1,0:T(8,128)(2,1)} copy(bf16[1,256,256]{2,1,0:T(8,128)(2,1)S(1)} %bitcast.18) | data formatting | bytes 262144
  58.3 0.7 %copy.20 = bf16[1,256,256]{2,1,0:T(8,128)(2,1)} copy(bf16[1,256,256]{2,1,0:T(8,128)(2,1)S(1)} %bitcast.17) | data formatting | bytes 262144
Async XLA Ops:
  0.6 0.7 %copy-start.5 = (s32[1,2]{1,0:T(1,128)S(1)}, s32[1,2]{1,0:T(1,128)}, u32[]{:S(2)}) copy-start(s32[1,2]{1,0:T(1,128)} %refresh_ref.1) | copy-start | bytes 28
  1.3 0.9 %copy-start = (f32[1,256,256]{2,1,0:T(8,128)S(1)}, f32[1,256,256]{2,1,0:T(8,128)}, u32[]{:S(2)}) copy-start(f32[1,256,256]{2,1,0:T(8,128)} %param.8) | copy-start | bytes 786436
  2.2 0.9 %copy-start.1 = (f32[1,256,256]{2,1,0:T(8,128)S(1)}, f32[1,256,256]{2,1,0:T(8,128)}, u32[]{:S(2)}) copy-start(f32[1,256,256]{2,1,0:T(8,128)} %param.9) | copy-start | bytes 786436
  3.2 0.9 %copy-start.2 = (bf16[128,2,256]{2,1,0:T(2,128)(2,1)S(1)}, bf16[128,2,256]{2,1,0:T(2,128)(2,1)}, u32[]{:S(2)}) copy-start(bf16[128,2,256]{2,1,0:T(2,128)(2,1)} %param.6) | copy-start | bytes 393220
  4.1 0.9 %copy-start.3 = (bf16[1,256,256]{2,1,0:T(8,128)(2,1)S(1)}, bf16[1,256,256]{2,1,0:T(8,128)(2,1)}, u32[]{:S(2)}) copy-start(bf16[1,256,256]{2,1,0:T(8,128)(2,1)} %param.10) | copy-start | bytes 393220
  5.0 0.9 %copy-start.4 = (bf16[1,256,256]{2,1,0:T(8,128)(2,1)S(1)}, bf16[1,256,256]{2,1,0:T(8,128)(2,1)}, u32[]{:S(2)}) copy-start(bf16[1,256,256]{2,1,0:T(8,128)(2,1)} %param.11) | copy-start | bytes 393220

commit v2 on v1

v2 whole, which is shorter than its diff:
```python
import jax
import jax.numpy as jnp
from jax import lax
from jax.experimental import pallas as pl
from jax.experimental.pallas import tpu as pltpu
from jax.sharding import PartitionSpec as P

ITERS = 5
B = 256
X, Y, Z, C = 8, 8, 8, 2
GROUP = Z * C * 2

decay_rate = 0.8
epsilon = 1e-06

f32, bf16 = jnp.float32, jnp.bfloat16
MESH = pl.DeviceIdType.MESH


def dot(a, b, dims=((1,), (0,))):
    return lax.dot_general(a, b, (dims, ((), ())), preferred_element_type=f32)


def split(a):
    high = a.astype(bf16)
    return high, (a - high.astype(f32)).astype(bf16)


def product(a, b):
    return dot(a[0], b[0]) + (dot(a[0], b[1]) + dot(a[1], b[0]))


def inverse_fourth_roots(stats):
    n = range(len(stats))
    rows = lax.broadcasted_iota(jnp.int32, (B, B), 0)
    on_diagonal = rows == lax.broadcasted_iota(jnp.int32, (B, B), 1)
    frobenius = [jnp.sqrt(jnp.sum(s * s, keepdims=True)) for s in stats]
    matrix = [stats[i] / frobenius[i] for i in n]
    root = None
    for sweep in range(ITERS):
        parts = [split(m) for m in matrix]
        if root is None:
            root = [jnp.where(on_diagonal, 1.25, 0.0) - 0.25 * m for m in matrix]
        else:
            root = [1.25 * root[i] - 0.25 * product(split(root[i]), parts[i]) for i in n]
        if sweep < ITERS - 1:
            square = [product(parts[i], parts[i]) for i in n]
            r = [(square[i] - 10.0 * matrix[i]) * 0.0625 for i in n]
            rp = [split(x) for x in r]
            r4 = [3.125 * r[i] + product(rp[i], rp[i]) for i in n]
            matrix = [2.44140625 * matrix[i] + product(split(r4[i]), parts[i]) for i in n]
    scale = [jnp.exp(-0.25 * jnp.log(c)) for c in frobenius]
    return [root[i] * scale[i] for i in n]


def kernel(
    refresh_ref, g_ref, ls_ref, rs_ref, lr_ref, rr_ref,
    out_ref, nl_ref, nr_ref, nlr_ref, nrr_ref,
    refresh, relay, relay_rows, block, pre, back, relay_back, ls, rs, lr, rr, nl, nr, nlr, nrr,
    load_sem, store_sem, send1, recv1, send2, recv2, send3, recv3, send4, recv4,
):
    me, x = lax.axis_index("fsdp"), lax.axis_index("own")
    y, z, c = me // (Z * C), (me // C) % Z, me % C
    y_to = (x + Y - y) % Y

    def at(px, py, pz, pc):
        return ((py * Z + pz) * C + pc, px)

    loads = [
        pltpu.make_async_copy(src, dst, load_sem.at[i])
        for i, (src, dst) in enumerate(
            ((refresh_ref, refresh), (ls_ref, ls), (rs_ref, rs), (lr_ref, lr), (rr_ref, rr))
        )
    ]

    peers = [((z + i) % Z, (c + j) % C) for i in range(Z) for j in range(C)][1:]
    barrier = pltpu.get_barrier_semaphore()

    def greet(device):
        pl.semaphore_signal(barrier, inc=1, device_id=device, device_id_type=MESH)

    for pz, pc in peers:
        greet(at(x, y, pz, pc))
    for i in range(1, X):
        px = (x + i) % X
        greet(at(px, (px + Y - y) % Y, z, c))

    @pl.when(y_to != y)
    def _():
        greet(at(x, y_to, z, c))

    for copy in loads:
        copy.start()
    pl.semaphore_wait(barrier, len(peers) + X - 1 + (y_to != y).astype(jnp.int32))

    def remote(src, dst, send, recv, to):
        pltpu.make_async_remote_copy(
            src_ref=src, dst_ref=dst, send_sem=send, recv_sem=recv, device_id=to, device_id_type=MESH
        ).start()

    def drained(ref, sem):
        pltpu.make_async_copy(ref, ref, sem).wait()

    def among_peers(src, dst, send, recv):
        for pz, pc in peers:
            remote(src.at[pz, pc], dst.at[z, c], send, recv, at(x, y, pz, pc))
        pltpu.make_async_copy(src.at[z, c], dst.at[z, c], recv).start()

    def to_replicas(src, dst, send, recv):
        for i in range(1, X):
            remote(src, dst, send, recv, at((x + i) % X, y_to, z, c))

        @pl.when(y_to != y)
        def _():
            remote(src, dst, send, recv, at(x, y_to, z, c))

        @pl.when(y_to == y)
        def _():
            pltpu.make_async_copy(src, dst, recv).start()

    def sent_to_peers(ref, sem):
        drained(ref.at[1:Z], sem)
        drained(ref.at[0, 0], sem)

    def sent_to_replicas(ref, sem):
        for i in range(1, X):
            drained(ref, sem)

        @pl.when(y_to != y)
        def _():
            drained(ref, sem)

    among_peers(g_ref.at[y_to], relay, send1, recv1)
    drained(relay, recv1)
    relay_rows[...] = relay[...].reshape(GROUP, B)
    to_replicas(relay_rows, block.at[pl.ds(pl.multiple_of(y * GROUP, GROUP), GROUP)], send2, recv2)
    for copy in loads:
        copy.wait()
    drained(block, recv2)

    g = block[...]
    new_left = decay_rate * ls[...] + (1.0 - decay_rate) * dot(g, g, ((1,), (1,)))
    new_right = decay_rate * rs[...] + (1.0 - decay_rate) * dot(g, g, ((0,), (0,)))
    nl[...] = new_left
    nr[...] = new_right
    stores = [
        pltpu.make_async_copy(src, dst, store_sem.at[i])
        for i, (src, dst) in enumerate(((nl, nl_ref), (nr, nr_ref), (nlr, nlr_ref), (nrr, nrr_ref)))
    ]
    stores[0].start()
    stores[1].start()
    left_fresh, right_fresh = inverse_fourth_roots([new_left, new_right])
    left = jnp.where(refresh[0, 0] == 1, left_fresh.astype(bf16), lr[...])
    right = jnp.where(refresh[0, 1] == 1, right_fresh.astype(bf16), rr[...])
    nlr[...] = left
    nrr[...] = right
    stores[2].start()
    stores[3].start()
    preconditioned = dot(dot(left, g).astype(bf16), right)
    pre[...] = preconditioned
    wide = g.astype(f32)
    grad_norm = jnp.sqrt(jnp.sum(wide * wide, keepdims=True))
    norm = jnp.sqrt(jnp.sum(preconditioned * preconditioned, keepdims=True) + epsilon)
    rows = pre[pl.ds(pl.multiple_of(y_to * GROUP, GROUP), GROUP), :]
    back[...] = (rows * (grad_norm / norm)).astype(bf16).reshape(Z, C, 2, B)

    among_peers(back, relay_back, send3, recv3)
    drained(relay_back, recv3)
    to_replicas(relay_back, out_ref.at[y], send4, recv4)

    sent_to_peers(relay, send1)
    sent_to_replicas(relay_rows, send2)
    sent_to_peers(back, send3)
    for copy in stores:
        copy.wait()
    sent_to_replicas(relay_back, send4)
    drained(out_ref, recv4)


def write_out(*refs):
    n = len(refs) // 2
    sem = refs[-1]
    copies = [pltpu.make_async_copy(refs[i], refs[n + i], sem.at[i]) for i in range(n)]
    for copy in copies:
        copy.start()
    for copy in copies:
        copy.wait()


def shards(gradient, refresh, left_stat, right_stat, left_root, right_root):
    anywhere = pl.BlockSpec(memory_space=pl.ANY)
    square = lambda dtype: jax.ShapeDtypeStruct((B, B), dtype)
    outs = (jax.ShapeDtypeStruct((Y, Z, C, 2, B), bf16), square(f32), square(f32), square(bf16), square(bf16))
    dma = pltpu.SemaphoreType.DMA
    results = pl.pallas_call(
        kernel,
        out_shape=outs,
        in_specs=[anywhere] * 6,
        out_specs=(anywhere,) * 5,
        scratch_shapes=[
            pltpu.SMEM((1, 2), jnp.int32),
            pltpu.VMEM((Z, C, 2, B), bf16),
            pltpu.VMEM((GROUP, B), bf16),
            pltpu.VMEM((B, B), bf16),
            pltpu.VMEM((B, B), f32),
            pltpu.VMEM((Z, C, 2, B), bf16),
            pltpu.VMEM((Z, C, 2, B), bf16),
        ]
        + [pltpu.VMEM((B, B), t) for t in (f32, f32, bf16, bf16, f32, f32, bf16, bf16)]
        + [dma((5,)), dma((4,))]
        + [dma] * 8,
        compiler_params=pltpu.CompilerParams(collective_id=0, has_side_effects=True),
    )(
        refresh, gradient.reshape(Y, Z, C, 2, B), left_stat[0], right_stat[0], left_root[0], right_root[0]
    )
    grafted, new_left, new_right, new_left_root, new_right_root = pl.pallas_call(
        write_out,
        out_shape=outs,
        in_specs=[anywhere] * 5,
        out_specs=(anywhere,) * 5,
        scratch_shapes=[dma((5,))],
    )(*results)
    return (
        grafted.reshape(Y * Z * C, 2, B), new_left[None], new_right[None], new_left_root[None], new_right_root[None]
    )


def solution(mesh):
    rows, blocks = P(None, "fsdp", None), P("fsdp", None, None)
    return jax.shard_map(
        shards,
        mesh=mesh,
        in_specs=(rows, P("fsdp", None), blocks, blocks, blocks, blocks),
        out_specs=(rows, blocks, blocks, blocks, blocks),
        check_vma=False,
    )
```

time: 59.2 us -> 83.1 us (1.40)
  Pallas kernels: 49.6 us -> 82 us
  local copies, waits for them, and re-layouts: 8.63 us -> 0 us
    pallas_call x1 -> x2, Pallas kernels: 49.6 us -> 82 us  [the longest x1 53.1 us: shards(): pl.pallas_call(kernel, out_shape=outs, in_specs=[anywhere] * 6, out_specs...]
    unnamed x17 -> x0, local copies, waits for them, and re-layouts: 8.63 us -> none
where the time goes in v2:
time: 83.1 us; the launch traced here: 82.6 us
  Pallas kernels  82 us (99%)
    pallas_call x1, Pallas kernels, shards(): pl.pallas_call(kernel, out_shape=outs, in_specs=[anywhere] * 6, out_specs...  53.1 us
    pallas_call x1, Pallas kernels, shards(): pl.pallas_call(write_out, out_shape=outs, in_specs=[anywhere] * 5, out_sp...  28.9 us

profile of v2, /device:TPU:1, one launch (start us, length us, event | category | flops | bytes accessed | tf_op | source)
XLA Modules:
  0.0 82.6 jit_solution(15437662177985412550)
XLA Ops:
  0.6 53.1 %shard_map.101 = (bf16[8,8,2,2,256]{4,3,2,1,0:T(2,128)(2,1)}, f32[256,256]{1,0:T(8,128)}, f32[256,256]{1,0:T(8,128)}, bf16[256,256]{1,0:T(8,128)(2,1)}, bf16[256,256]{1,0:T(8,128)(2,1)}) custom-call(s32[1,2]{1,0:T(1,128)} %refresh_ref.1, bf16[8,8,2,2,256]{4,3,2,1,0:T(2,128)(2,1)} %bitcast.12, f32[256,256]{1,0:T(8,128)} %bitcast.10, f32[256,256]{1,0:T(8,128)} %bitcast.11, ...), custom_call_target="tpu_custom_call" | custom-call | tf_op jit(solution)/shard_map/pallas_call | solution.py:195
  53.7 28.9 %shard_map.102 = (bf16[8,8,2,2,256]{4,3,2,1,0:T(2,128)(2,1)}, f32[256,256]{1,0:T(8,128)}, f32[256,256]{1,0:T(8,128)}, bf16[256,256]{1,0:T(8,128)(2,1)}, bf16[256,256]{1,0:T(8,128)(2,1)}) custom-call(bf16[8,8,2,2,256]{4,3,2,1,0:T(2,128)(2,1)} %get-tuple-element.15.refs_0_, f32[256,256]{1,0:T(8,128)} %get-tuple-element.16.refs_1_, ...), custom_call_target="tpu_custom_call" | custom-call | tf_op jit(solution)/shard_map/pallas_call | solution.py:216

commit v3 on v2

v3 whole, which is shorter than its diff:
```python
import jax
import jax.numpy as jnp
from jax import lax
from jax.experimental import pallas as pl
from jax.experimental.pallas import tpu as pltpu
from jax.sharding import PartitionSpec as P

ITERS = 5
B = 256
Y, Z, C = 8, 8, 2

decay_rate = 0.8
epsilon = 1e-06

f32, bf16 = jnp.float32, jnp.bfloat16
MESH = pl.DeviceIdType.MESH


def dot(a, b, dims=((1,), (0,))):
    return lax.dot_general(a, b, (dims, ((), ())), preferred_element_type=f32)


def split(a):
    high = a.astype(bf16)
    return high, (a - high.astype(f32)).astype(bf16)


def product(a, b):
    return dot(a[0], b[0]) + (dot(a[0], b[1]) + dot(a[1], b[0]))


def inverse_fourth_roots(stats):
    n = range(len(stats))
    rows = lax.broadcasted_iota(jnp.int32, (B, B), 0)
    on_diagonal = rows == lax.broadcasted_iota(jnp.int32, (B, B), 1)
    frobenius = [jnp.sqrt(jnp.sum(s * s, keepdims=True)) for s in stats]
    matrix = [stats[i] / frobenius[i] for i in n]
    root = None
    for sweep in range(ITERS):
        parts = [split(m) for m in matrix]
        if root is None:
            root = [jnp.where(on_diagonal, 1.25, 0.0) - 0.25 * m for m in matrix]
        else:
            root = [1.25 * root[i] - 0.25 * product(split(root[i]), parts[i]) for i in n]
        if sweep < ITERS - 1:
            square = [product(parts[i], parts[i]) for i in n]
            r = [(square[i] - 10.0 * matrix[i]) * 0.0625 for i in n]
            rp = [split(x) for x in r]
            r4 = [3.125 * r[i] + product(rp[i], rp[i]) for i in n]
            matrix = [2.44140625 * matrix[i] + product(split(r4[i]), parts[i]) for i in n]
    scale = [jnp.exp(-0.25 * jnp.log(c)) for c in frobenius]
    return [root[i] * scale[i] for i in n]


def kernel(
    refresh_ref, g_ref, ls_ref, rs_ref, lr_ref, rr_ref,
    out_ref, nl_ref, nr_ref, nlr_ref, nrr_ref,
    refresh, relay, block, back, relay_back, sorted_back, landed, ls, rs, lr, rr, nl, nr, nlr, nrr,
    load_sem, store_sem, send1, recv1, send2, recv2, send3, recv3, send4, recv4, here,
):
    me, own = lax.axis_index("fsdp"), lax.axis_index("own")
    y, z, c = me // (Z * C), (me // C) % Z, me % C

    def at(py, pz, pc):
        return ((py * Z + pz) * C + pc, own)

    loads = [
        pltpu.make_async_copy(src, dst, load_sem.at[i])
        for i, (src, dst) in enumerate(
            ((refresh_ref, refresh), (ls_ref, ls), (rs_ref, rs), (lr_ref, lr), (rr_ref, rr))
        )
    ]

    row = [((y + i) % Y, (c + j) % C) for i in range(Y) for j in range(C)][1:]
    barrier = pltpu.get_barrier_semaphore()
    for py, pc in row:
        pl.semaphore_signal(barrier, inc=1, device_id=at(py, z, pc), device_id_type=MESH)
    for pz in range(1, Z):

        @pl.when(pz > z)
        def _():
            pl.semaphore_signal(barrier, inc=1, device_id=at(y, pz, c), device_id_type=MESH)

    for copy in loads:
        copy.start()
    pl.semaphore_wait(barrier, len(row) + z)
    for pz in range(Z - 1):

        @pl.when(pz < z)
        def _():
            pl.semaphore_signal(here.at[z], inc=1, device_id=at(y, pz, c), device_id_type=MESH)

    def remote(src, dst, send, recv, to):
        pltpu.make_async_remote_copy(
            src_ref=src, dst_ref=dst, send_sem=send, recv_sem=recv, device_id=to, device_id_type=MESH
        ).start()

    def drained(ref, sem):
        pltpu.make_async_copy(ref, ref, sem).wait()

    for py, pc in row[::-1]:
        remote(g_ref.at[py, :, pc], relay.at[:, y, c], send1, recv1, at(py, z, pc))
    pltpu.make_async_copy(g_ref.at[y, :, c], relay.at[:, y, c], recv1).start()
    drained(relay, recv1)

    for pz in range(Z):

        @pl.when(pz > z)
        def _():
            pl.semaphore_wait(here.at[pz], 1)

        @pl.when(pz != z)
        def _():
            remote(relay.at[pz], block.at[:, z], send2, recv2, at(y, pz, c))

    pltpu.make_async_copy(relay.at[z], block.at[:, z], recv2).start()
    for copy in loads:
        copy.wait()
    drained(block, recv2)

    g = block[...].reshape(B, B)
    new_left = decay_rate * ls[...] + (1.0 - decay_rate) * dot(g, g, ((1,), (1,)))
    new_right = decay_rate * rs[...] + (1.0 - decay_rate) * dot(g, g, ((0,), (0,)))
    nl[...] = new_left
    nr[...] = new_right
    stores = [
        pltpu.make_async_copy(src, dst, store_sem.at[i])
        for i, (src, dst) in enumerate(((nl, nl_ref), (nr, nr_ref), (nlr, nlr_ref), (nrr, nrr_ref)))
    ]
    stores[0].start()
    stores[1].start()
    left_fresh, right_fresh = inverse_fourth_roots([new_left, new_right])
    left = jnp.where(refresh[0, 0] == 1, left_fresh.astype(bf16), lr[...])
    right = jnp.where(refresh[0, 1] == 1, right_fresh.astype(bf16), rr[...])
    nlr[...] = left
    nrr[...] = right
    stores[2].start()
    stores[3].start()
    preconditioned = dot(dot(left, g).astype(bf16), right)
    wide = g.astype(f32)
    grad_norm = jnp.sqrt(jnp.sum(wide * wide, keepdims=True))
    norm = jnp.sqrt(jnp.sum(preconditioned * preconditioned, keepdims=True) + epsilon)
    grafted = (preconditioned * (grad_norm / norm)).astype(bf16)
    back[...] = grafted.reshape(Y, Z, C, 2, B)

    for i in (4, 3, 5, 2, 6, 1, 7):
        py = (y + i) % Y
        remote(back.at[py], relay_back.at[y], send3, recv3, at(py, z, c))
    pltpu.make_async_copy(back.at[y], relay_back.at[y], recv3).start()
    drained(relay_back, recv3)

    for pz in range(Z):
        for pc in range(C):
            sorted_back[pz, pc] = relay_back[:, pz, pc]

            @pl.when((pz != z) | (pc != c))
            def _():
                remote(sorted_back.at[pz, pc], landed.at[z, c], send4, recv4, at(y, pz, pc))

    pltpu.make_async_copy(sorted_back.at[z, c], landed.at[z, c], recv4).start()

    drained(relay.at[1:], send1)
    drained(relay.at[0, 0:4], send1)
    drained(block.at[1:], send2)
    drained(relay_back.at[1:], send3)
    for copy in stores:
        copy.wait()
    drained(landed, recv4)
    out_ref[...] = landed[...]
    drained(landed.at[1:], send4)
    drained(landed.at[0, 0], send4)


def write_out(rows_ref, nl_in, nr_in, nlr_in, nrr_in, out_ref, nl_ref, nr_ref, nlr_ref, nrr_ref, sem):
    copies = [pltpu.make_async_copy(rows_ref.at[:, :, y], out_ref.at[y], sem.at[y]) for y in range(Y)]
    copies += [
        pltpu.make_async_copy(src, dst, sem.at[Y + i])
        for i, (src, dst) in enumerate(((nl_in, nl_ref), (nr_in, nr_ref), (nlr_in, nlr_ref), (nrr_in, nrr_ref)))
    ]
    for copy in copies:
        copy.start()
    for copy in copies:
        copy.wait()


def shards(gradient, refresh, left_stat, right_stat, left_root, right_root):
    anywhere = pl.BlockSpec(memory_space=pl.ANY)
    vmem = pl.BlockSpec(memory_space=pltpu.VMEM)
    square = lambda dtype: jax.ShapeDtypeStruct((B, B), dtype)
    squares = (square(f32), square(f32), square(bf16), square(bf16))
    rows = (Y, Z, C, 2, B)
    dma = pltpu.SemaphoreType.DMA
    operands = (
        refresh, gradient.reshape(rows), left_stat[0], right_stat[0], left_root[0], right_root[0]
    )
    results = pl.pallas_call(
        kernel,
        out_shape=(jax.ShapeDtypeStruct((Z, C, Y, 2, B), bf16),) + squares,
        in_specs=[anywhere] * 6,
        out_specs=(vmem,) + (anywhere,) * 4,
        scratch_shapes=[pltpu.SMEM((1, 2), jnp.int32)]
        + [pltpu.VMEM(r, bf16) for r in ((Z, Y, C, 2, B), rows, rows, rows, (Z, C, Y, 2, B), (Z, C, Y, 2, B))]
        + [pltpu.VMEM((B, B), t) for t in (f32, f32, bf16, bf16, f32, f32, bf16, bf16)]
        + [dma((5,)), dma((4,))]
        + [dma] * 8
        + [pltpu.SemaphoreType.REGULAR((Z,))],
        compiler_params=pltpu.CompilerParams(
            collective_id=0, has_side_effects=True, vmem_limit_bytes=32 * 1024 * 1024
        ),
    )(*[pltpu.with_memory_space_constraint(x, pltpu.HBM) for x in operands])
    grafted, new_left, new_right, new_left_root, new_right_root = pl.pallas_call(
        write_out,
        out_shape=(jax.ShapeDtypeStruct(rows, bf16),) + squares,
        in_specs=[vmem] * 5,
        out_specs=(anywhere,) * 5,
        scratch_shapes=[dma((Y + 4,))],
        compiler_params=pltpu.CompilerParams(vmem_limit_bytes=32 * 1024 * 1024),
    )(*results)
    return (
        grafted.reshape(Y * Z * C, 2, B), new_left[None], new_right[None], new_left_root[None], new_right_root[None]
    )


def solution(mesh):
    rows, blocks = P(None, "fsdp", None), P("fsdp", None, None)
    return jax.shard_map(
        shards,
        mesh=mesh,
        in_specs=(rows, P("fsdp", None), blocks, blocks, blocks, blocks),
        out_specs=(rows, blocks, blocks, blocks, blocks),
        check_vma=False,
    )
```

time: 83.1 us -> 49.9 us (0.60)
  Pallas kernels: 82 us -> 49.1 us
    pallas_call x2, Pallas kernels: 82 us -> 49.1 us  [the longest x1 48.1 us: shards(): pl.pallas_call(kernel, out_shape=(jax.ShapeDtypeStruct((Z, C, Y, 2, B), b...]
where the time goes in v3:
time: 49.9 us; the launch traced here: 49.8 us
  Pallas kernels  49.1 us (98%)
  between operations  0.64 us (1%)
    pallas_call x1, Pallas kernels, shards(): pl.pallas_call(kernel, out_shape=(jax.ShapeDtypeStruct((Z, C, Y, 2, B), b...  48.1 us
    pallas_call x1, Pallas kernels, shards(): pl.pallas_call(write_out, out_shape=(jax.ShapeDtypeStruct(rows, bf16),) +...  1.02 us

profile of v3, /device:TPU:1, one launch (start us, length us, event | category | flops | bytes accessed | tf_op | source)
XLA Modules:
  0.0 49.8 jit_solution(846952207815999239)
XLA Ops:
  0.6 48.1 %shard_map.101 = (bf16[8,2,8,2,256]{4,3,2,1,0:T(2,128)(2,1)S(1)}, f32[256,256]{1,0:T(8,128)S(1)}, f32[256,256]{1,0:T(8,128)S(1)}, bf16[256,256]{1,0:T(8,128)(2,1)S(1)}, bf16[256,256]{1,0:T(8,128)(2,1)S(1)}) custom-call(s32[1,2]{1,0:T(1,128)} %refresh_ref.1, bf16[8,8,2,2,256]{4,3,2,1,0:T(2,128)(2,1)} %bitcast.12, f32[256,256]{1,0:T(8,128)} %bitcast.10, ...), custom_call_target="tpu_custom_call" | custom-call | tf_op jit(solution)/shard_map/pallas_call | solution.py:196
  48.7 1.0 %shard_map.102 = (bf16[8,8,2,2,256]{4,3,2,1,0:T(2,128)(2,1)}, f32[256,256]{1,0:T(8,128)}, f32[256,256]{1,0:T(8,128)}, bf16[256,256]{1,0:T(8,128)(2,1)}, bf16[256,256]{1,0:T(8,128)(2,1)}) custom-call(bf16[8,2,8,2,256]{4,3,2,1,0:T(2,128)(2,1)S(1)} %get-tuple-element.15.rows_ref, f32[256,256]{1,0:T(8,128)S(1)} %get-tuple-element.16.nl_in, ...), custom_call_target="tpu_custom_call" | custom-call | tf_op jit(solution)/shard_map/pallas_call | solution.py:211

commit v4 on v3

v4 whole, which is shorter than its diff:
```python
import functools

import jax
import jax.numpy as jnp
from jax import lax
from jax.experimental import pallas as pl
from jax.experimental.pallas import tpu as pltpu
from jax.sharding import PartitionSpec as P

ITERS = 5
B = 256
Y, Z, C = 8, 8, 2

decay_rate = 0.8
epsilon = 1e-06

f32, bf16 = jnp.float32, jnp.bfloat16
MESH = pl.DeviceIdType.MESH


def dot(a, b, dims=((1,), (0,))):
    return lax.dot_general(a, b, (dims, ((), ())), preferred_element_type=f32)


def split(a):
    high = a.astype(bf16)
    return high, (a - high.astype(f32)).astype(bf16)


def product(a, b):
    return dot(a[0], b[0]) + (dot(a[0], b[1]) + dot(a[1], b[0]))


def inverse_fourth_roots(stats):
    n = range(len(stats))
    rows = lax.broadcasted_iota(jnp.int32, (B, B), 0)
    on_diagonal = rows == lax.broadcasted_iota(jnp.int32, (B, B), 1)
    frobenius = [jnp.sqrt(jnp.sum(s * s, keepdims=True)) for s in stats]
    matrix = [stats[i] / frobenius[i] for i in n]
    root = None
    for sweep in range(ITERS):
        parts = [split(m) for m in matrix]
        if root is None:
            root = [jnp.where(on_diagonal, 1.25, 0.0) - 0.25 * m for m in matrix]
        else:
            root = [1.25 * root[i] - 0.25 * product(split(root[i]), parts[i]) for i in n]
        if sweep < ITERS - 1:
            square = [product(parts[i], parts[i]) for i in n]
            r = [(square[i] - 10.0 * matrix[i]) * 0.0625 for i in n]
            rp = [split(x) for x in r]
            r4 = [3.125 * r[i] + product(rp[i], rp[i]) for i in n]
            matrix = [2.44140625 * matrix[i] + product(split(r4[i]), parts[i]) for i in n]
    scale = [jnp.exp(-0.25 * jnp.log(c)) for c in frobenius]
    return [root[i] * scale[i] for i in n]


def kernel(
    refresh_ref, g_ref, ls_ref, rs_ref, lr_ref, rr_ref,
    out_ref, nl_ref, nr_ref, nlr_ref, nrr_ref,
    refresh, both, relay, block, back, both_back, ls, rs, lr, rr, nl, nr, nlr, nrr,
    load_sem, store_sem, send_core, recv_core, send_row, send_down, send_up, recv_relay, recv_block,
    send_back, recv_back, send_out, recv_out, here_row, here_up,
):
    me, own = lax.axis_index("fsdp"), lax.axis_index("own")
    y, z, c = me // (Z * C), (me // C) % Z, me % C
    ORDER = (0, 1, 2, 3, 6, 7, 4, 5)
    rank = jnp.where(y < 4, y, (y + 2) % 4 + 4)

    def at(py, pz, pc=c):
        return ((py * Z + pz) * C + pc, own)

    def signal(sem, device):
        pl.semaphore_signal(sem, inc=1, device_id=device, device_id_type=MESH)

    def remote(src, dst, send, recv, to):
        pltpu.make_async_remote_copy(
            src_ref=src, dst_ref=dst, send_sem=send, recv_sem=recv, device_id=to, device_id_type=MESH
        ).start()

    def local(src, dst, sem):
        pltpu.make_async_copy(src, dst, sem).start()

    def drained(ref, sem):
        pltpu.make_async_copy(ref, ref, sem).wait()

    def repeat(low, high, body):
        def step(i, carry):
            body(i)
            return carry

        lax.fori_loop(low, high, step, 0)

    barrier = pltpu.get_barrier_semaphore()
    signal(barrier, at(y, z, 1 - c))
    for r in range(1, Y):

        @pl.when(r > rank)
        def _():
            signal(barrier, at(ORDER[r], z))

    @functools.partial(repeat, z + 1, Z)
    def _(pz):
        for py in range(Y):
            signal(barrier, at(py, pz))

    loads = [
        pltpu.make_async_copy(src, dst, load_sem.at[i])
        for i, (src, dst) in enumerate(
            ((refresh_ref, refresh), (ls_ref, ls), (rs_ref, rs), (lr_ref, lr), (rr_ref, rr))
        )
    ]
    for copy in loads:
        copy.start()
    pl.semaphore_wait(barrier, 1 + rank + Y * z)
    for r in range(Y - 1):

        @pl.when(r < rank)
        def _():
            signal(here_row.at[rank], at(ORDER[r], z))

    @functools.partial(repeat, 0, z)
    def _(pz):
        signal(here_up.at[z], at(y, pz))

    remote(g_ref.at[:, :, 1 - c], both.at[:, :, c], send_core, recv_core, at(y, z, 1 - c))
    local(g_ref.at[:, :, c], both.at[:, :, c], recv_core)
    drained(both, recv_core)

    def to_row(py):
        remote(both.at[py, z], block.at[y, z], send_row, recv_block, at(py, z))

        @functools.partial(repeat, z + 1, Z)
        def _(pz):
            remote(both.at[py, pz], relay.at[pz, y], send_row, recv_relay.at[pz], at(py, z))

    for r in range(Y - 1):

        @pl.when(r < rank)
        def _():
            to_row(ORDER[r])

    def to_lower(pz):
        for py in range(Y):
            remote(both.at[py, pz], block.at[y, z], send_down, recv_block, at(py, pz))

    @functools.partial(repeat, 0, z)
    def _(i):
        to_lower(lax.rem(i + z // 2, z))

    local(both.at[y, z], block.at[y, z], recv_block)

    @functools.partial(repeat, z + 1, Z)
    def _(pz):
        local(both.at[y, pz], relay.at[pz, y], recv_relay.at[pz])

    for r in range(1, Y):

        @pl.when(r > rank)
        def _():
            pl.semaphore_wait(here_row.at[r], 1)
            to_row(ORDER[r])

    @functools.partial(repeat, z + 1, Z)
    def _(pz):
        drained(relay.at[pz], recv_relay.at[pz])
        pl.semaphore_wait(here_up.at[pz], 1)
        remote(relay.at[pz], block.at[:, z], send_up, recv_block, at(y, pz))

    drained(both.at[:, :, 0], send_core)
    repeat(z, Z, lambda i: drained(relay.at[0, 1:], send_row))
    repeat(0, z, lambda i: drained(relay.at[0], send_down))
    repeat(z + 1, Z, lambda i: drained(relay.at[0], send_up))
    for copy in loads:
        copy.wait()
    drained(block, recv_block)

    g = block[...].reshape(B, B)
    new_left = decay_rate * ls[...] + (1.0 - decay_rate) * dot(g, g, ((1,), (1,)))
    new_right = decay_rate * rs[...] + (1.0 - decay_rate) * dot(g, g, ((0,), (0,)))
    nl[...] = new_left
    nr[...] = new_right
    stores = [
        pltpu.make_async_copy(src, dst, store_sem.at[i])
        for i, (src, dst) in enumerate(((nl, nl_ref), (nr, nr_ref), (nlr, nlr_ref), (nrr, nrr_ref)))
    ]
    stores[0].start()
    stores[1].start()
    left_fresh, right_fresh = inverse_fourth_roots([new_left, new_right])
    left = jnp.where(refresh[0, 0] == 1, left_fresh.astype(bf16), lr[...])
    right = jnp.where(refresh[0, 1] == 1, right_fresh.astype(bf16), rr[...])
    nlr[...] = left
    nrr[...] = right
    stores[2].start()
    stores[3].start()
    preconditioned = dot(dot(left, g).astype(bf16), right)
    wide = g.astype(f32)
    grad_norm = jnp.sqrt(jnp.sum(wide * wide, keepdims=True))
    norm = jnp.sqrt(jnp.sum(preconditioned * preconditioned, keepdims=True) + epsilon)
    grafted = (preconditioned * (grad_norm / norm)).astype(bf16)
    back[...] = grafted.reshape(Y, Z, C, 2, B)

    remote(back.at[:, :, 1 - c], both_back.at[:, :, c], send_back, recv_back, at(y, z, 1 - c))
    local(back.at[:, :, c], both_back.at[:, :, c], recv_back)
    drained(both_back, recv_back)

    @functools.partial(repeat, 0, Z)
    def _(pz):
        for i in (4, 3, 5, 2, 6, 1, 7):
            py = (y + i) % Y
            remote(both_back.at[py, pz], out_ref.at[y, z], send_out, recv_out, at(py, pz))

        @pl.when(pz != z)
        def _():
            remote(both_back.at[y, pz], out_ref.at[y, z], send_out, recv_out, at(y, pz))

    local(both_back.at[y, z], out_ref.at[y, z], recv_out)
    drained(both_back.at[:, :, 0], send_back)
    for copy in stores:
        copy.wait()
    drained(out_ref, recv_out)
    drained(both_back.at[1:], send_out)
    drained(both_back.at[0, 1:], send_out)


def write_out(*refs):
    n = len(refs) // 2
    copies = [pltpu.make_async_copy(refs[i], refs[n + i], refs[-1].at[i]) for i in range(n)]
    for copy in copies:
        copy.start()
    for copy in copies:
        copy.wait()


def shards(gradient, refresh, left_stat, right_stat, left_root, right_root):
    anywhere = pl.BlockSpec(memory_space=pl.ANY)
    square = lambda dtype: jax.ShapeDtypeStruct((B, B), dtype)
    rows = (Y, Z, C, 2, B)
    outs = (jax.ShapeDtypeStruct(rows, bf16), square(f32), square(f32), square(bf16), square(bf16))
    dma, regular = pltpu.SemaphoreType.DMA, pltpu.SemaphoreType.REGULAR
    operands = (
        refresh, gradient.reshape(rows), left_stat[0], right_stat[0], left_root[0], right_root[0]
    )
    results = pl.pallas_call(
        kernel,
        out_shape=outs,
        in_specs=[anywhere] * 6,
        out_specs=(anywhere,) * 5,
        scratch_shapes=[pltpu.SMEM((1, 2), jnp.int32)]
        + [pltpu.VMEM(r, bf16) for r in (rows, (Z, Y, C, 2, B), rows, rows, rows)]
        + [pltpu.VMEM((B, B), t) for t in (f32, f32, bf16, bf16, f32, f32, bf16, bf16)]
        + [dma((5,)), dma((4,)), dma, dma, dma, dma, dma, dma((Z,)), dma, dma, dma, dma, dma]
        + [regular((Y,)), regular((Z,))],
        compiler_params=pltpu.CompilerParams(
            collective_id=0, has_side_effects=True, vmem_limit_bytes=32 * 1024 * 1024
        ),
    )(*[pltpu.with_memory_space_constraint(x, pltpu.HBM) for x in operands])
    grafted, new_left, new_right, new_left_root, new_right_root = pl.pallas_call(
        write_out,
        out_shape=outs,
        in_specs=[pl.BlockSpec(memory_space=pltpu.VMEM)] * 5,
        out_specs=(anywhere,) * 5,
        scratch_shapes=[dma((5,))],
        compiler_params=pltpu.CompilerParams(vmem_limit_bytes=32 * 1024 * 1024),
    )(*results)
    return (
        grafted.reshape(Y * Z * C, 2, B), new_left[None], new_right[None], new_left_root[None], new_right_root[None]
    )


def solution(mesh):
    rows, blocks = P(None, "fsdp", None), P("fsdp", None, None)
    return jax.shard_map(
        shards,
        mesh=mesh,
        in_specs=(rows, P("fsdp", None), blocks, blocks, blocks, blocks),
        out_specs=(rows, blocks, blocks, blocks, blocks),
        check_vma=False,
    )
```

time: 49.9 us -> 47.2 us (0.946)
  Pallas kernels: 49.1 us -> 46.4 us
    pallas_call x2, Pallas kernels: 49.1 us -> 46.4 us  [the longest x1 45.4 us: shards(): pl.pallas_call(kernel, out_shape=outs, in_specs=[anywhere] * 6, out_specs...]
where the time goes in v4:
time: 47.2 us; the launch traced here: 47 us
  Pallas kernels  46.4 us (98%)
  between operations  0.64 us (1%)
    pallas_call x1, Pallas kernels, shards(): pl.pallas_call(kernel, out_shape=outs, in_specs=[anywhere] * 6, out_specs...  45.4 us
    pallas_call x1, Pallas kernels, shards(): pl.pallas_call(write_out, out_shape=outs, in_specs=[pl.BlockSpec(memory_s...  0.96 us

profile of v4, /device:TPU:1, one launch (start us, length us, event | category | flops | bytes accessed | tf_op | source)
XLA Modules:
  0.0 47.0 jit_solution(7022360980991280649)
XLA Ops:
  0.6 45.4 %shard_map.101 = (bf16[8,8,2,2,256]{4,3,2,1,0:T(2,128)(2,1)S(1)}, f32[256,256]{1,0:T(8,128)S(1)}, f32[256,256]{1,0:T(8,128)S(1)}, bf16[256,256]{1,0:T(8,128)(2,1)S(1)}, bf16[256,256]{1,0:T(8,128)(2,1)S(1)}) custom-call(s32[1,2]{1,0:T(1,128)} %refresh_ref.1, bf16[8,8,2,2,256]{4,3,2,1,0:T(2,128)(2,1)} %bitcast.12, f32[256,256]{1,0:T(8,128)} %bitcast.10, ...), custom_call_target="tpu_custom_call" | custom-call | tf_op jit(solution)/shard_map/pallas_call | solution.py:243
  46.1 1.0 %shard_map.102 = (bf16[8,8,2,2,256]{4,3,2,1,0:T(2,128)(2,1)}, f32[256,256]{1,0:T(8,128)}, f32[256,256]{1,0:T(8,128)}, bf16[256,256]{1,0:T(8,128)(2,1)}, bf16[256,256]{1,0:T(8,128)(2,1)}) custom-call(bf16[8,8,2,2,256]{4,3,2,1,0:T(2,128)(2,1)S(1)} %get-tuple-element.15.refs_0_, f32[256,256]{1,0:T(8,128)S(1)} %get-tuple-element.16.refs_1_, ...), custom_call_target="tpu_custom_call" | custom-call | tf_op jit(solution)/shard_map/pallas_call | solution.py:257

commit v5 on v4

--- a/solution.py
+++ b/solution.py
@@ -22,13 +22,14 @@
     return lax.dot_general(a, b, (dims, ((), ())), preferred_element_type=f32)
 
 
-def split(a):
+def split(a, wide):
     high = a.astype(bf16)
-    return high, (a - high.astype(f32)).astype(bf16)
+    return (high, (a - high.astype(f32)).astype(bf16)) if wide else (high,)
 
 
 def product(a, b):
-    return dot(a[0], b[0]) + (dot(a[0], b[1]) + dot(a[1], b[0]))
+    high = dot(a[0], b[0])
+    return high if len(a) == 1 else high + (dot(a[0], b[1]) + dot(a[1], b[0]))
 
 
 def inverse_fourth_roots(stats):
@@ -36,20 +37,21 @@
     rows = lax.broadcasted_iota(jnp.int32, (B, B), 0)
     on_diagonal = rows == lax.broadcasted_iota(jnp.int32, (B, B), 1)
     frobenius = [jnp.sqrt(jnp.sum(s * s, keepdims=True)) for s in stats]
-    matrix = [stats[i] / frobenius[i] for i in n]
+    m = [stats[i] * (0.25 / frobenius[i]) for i in n]
     root = None
     for sweep in range(ITERS):
-        parts = [split(m) for m in matrix]
+        wide = sweep >= ITERS - 2
+        parts = [split(x, wide) for x in m]
+        if sweep < ITERS - 1:
+            r = [dot(parts[i][0], parts[i][0]) - 2.5 * m[i] for i in n]
         if root is None:
-            root = [jnp.where(on_diagonal, 1.25, 0.0) - 0.25 * m for m in matrix]
+            root = [jnp.where(on_diagonal, 1.25, 0.0) - x for x in m]
         else:
-            root = [1.25 * root[i] - 0.25 * product(split(root[i]), parts[i]) for i in n]
+            root = [1.25 * root[i] - product(split(root[i], wide), parts[i]) for i in n]
         if sweep < ITERS - 1:
-            square = [product(parts[i], parts[i]) for i in n]
-            r = [(square[i] - 10.0 * matrix[i]) * 0.0625 for i in n]
-            rp = [split(x) for x in r]
-            r4 = [3.125 * r[i] + product(rp[i], rp[i]) for i in n]
-            matrix = [2.44140625 * matrix[i] + product(split(r4[i]), parts[i]) for i in n]
+            high = [x.astype(bf16) for x in r]
+            r4 = [3.125 * r[i] + dot(high[i], high[i]) for i in n]
+            m = [2.44140625 * m[i] + product(split(r4[i], wide), parts[i]) for i in n]
     scale = [jnp.exp(-0.25 * jnp.log(c)) for c in frobenius]
     return [root[i] * scale[i] for i in n]
 
@@ -59,12 +61,18 @@
     out_ref, nl_ref, nr_ref, nlr_ref, nrr_ref,
     refresh, both, relay, block, back, both_back, ls, rs, lr, rr, nl, nr, nlr, nrr,
     load_sem, store_sem, send_core, recv_core, send_row, send_down, send_up, recv_relay, recv_block,
-    send_back, recv_back, send_out, recv_out, here_row, here_up,
+    send_back, recv_back, send_out, recv_out, here_row, here_up, here_corner,
 ):
     me, own = lax.axis_index("fsdp"), lax.axis_index("own")
     y, z, c = me // (Z * C), (me // C) % Z, me % C
     ORDER = (0, 1, 2, 3, 6, 7, 4, 5)
-    rank = jnp.where(y < 4, y, (y + 2) % 4 + 4)
+    rank = (jnp.where(y < 4, y, (y + 2) % 4 + 4) + jnp.where(z == 0, Y - 1, 0)) % Y
+    plane = (own == 0) & (c == 0)
+    corner = plane & (y == 0) & (z == 0)
+    between = plane & (z > 0) & (z < Z - 1)
+
+    def ordered(r):
+        return jnp.where(z == 0, ORDER[(r + 1) % Y], ORDER[r])
 
     def at(py, pz, pc=c):
         return ((py * Z + pz) * C + pc, own)
@@ -96,12 +104,16 @@
 
         @pl.when(r > rank)
         def _():
-            signal(barrier, at(ORDER[r], z))
-
-    @functools.partial(repeat, z + 1, Z)
+            signal(barrier, at(ordered(r), z))
+
+    @functools.partial(repeat, jnp.where(corner, Z - 1, z + 1), Z)
     def _(pz):
         for py in range(Y):
             signal(barrier, at(py, pz))
+
+    @pl.when(between)
+    def _():
+        signal(barrier, at(0, 0))
 
     loads = [
         pltpu.make_async_copy(src, dst, load_sem.at[i])
@@ -111,16 +123,24 @@
     ]
     for copy in loads:
         copy.start()
-    pl.semaphore_wait(barrier, 1 + rank + Y * z)
+    greetings = 1 + rank + Y * z - between.astype(jnp.int32)
+    pl.semaphore_wait(barrier, jnp.where(corner, 1 + rank + Y * (Z - 2), greetings))
     for r in range(Y - 1):
 
         @pl.when(r < rank)
         def _():
-            signal(here_row.at[rank], at(ORDER[r], z))
-
-    @functools.partial(repeat, 0, z)
+            signal(here_row.at[rank], at(ordered(r), z))
+
+    @functools.partial(repeat, (between & (y == 0)).astype(jnp.int32), z)
     def _(pz):
         signal(here_up.at[z], at(y, pz))
+
+    @pl.when(corner)
+    def _():
+        @functools.partial(repeat, 1, Z - 1)
+        def _(pz):
+            for py in range(Y):
+                signal(here_corner, at(py, pz))
 
     remote(g_ref.at[:, :, 1 - c], both.at[:, :, c], send_core, recv_core, at(y, z, 1 - c))
     local(g_ref.at[:, :, c], both.at[:, :, c], recv_core)
@@ -137,15 +157,20 @@
 
         @pl.when(r < rank)
         def _():
-            to_row(ORDER[r])
-
-    def to_lower(pz):
-        for py in range(Y):
-            remote(both.at[py, pz], block.at[y, z], send_down, recv_block, at(py, pz))
-
-    @functools.partial(repeat, 0, z)
-    def _(i):
-        to_lower(lax.rem(i + z // 2, z))
+            to_row(ordered(r))
+
+    def down(py, pz):
+        remote(both.at[py, pz], block.at[y, z], send_down, recv_block, at(py, pz))
+
+    for pz in (3, 4, 0, 5, 2, 1, 6):
+
+        @pl.when(pz < z)
+        def _():
+            for py in range(Y):
+                if py or pz:
+                    down(py, pz)
+                else:
+                    pl.when(jnp.logical_not(between))(functools.partial(down, 0, 0))
 
     local(both.at[y, z], block.at[y, z], recv_block)
 
@@ -158,12 +183,21 @@
         @pl.when(r > rank)
         def _():
             pl.semaphore_wait(here_row.at[r], 1)
-            to_row(ORDER[r])
+            to_row(ordered(r))
+
+    @pl.when(between)
+    def _():
+        pl.semaphore_wait(here_corner, 1)
+        down(0, 0)
 
     @functools.partial(repeat, z + 1, Z)
     def _(pz):
         drained(relay.at[pz], recv_relay.at[pz])
-        pl.semaphore_wait(here_up.at[pz], 1)
+
+        @pl.when(jnp.logical_not(corner) | (pz == Z - 1))
+        def _():
+            pl.semaphore_wait(here_up.at[pz], 1)
+
         remote(relay.at[pz], block.at[:, z], send_up, recv_block, at(y, pz))
 
     drained(both.at[:, :, 0], send_core)
@@ -249,7 +283,7 @@
         + [pltpu.VMEM(r, bf16) for r in (rows, (Z, Y, C, 2, B), rows, rows, rows)]
         + [pltpu.VMEM((B, B), t) for t in (f32, f32, bf16, bf16, f32, f32, bf16, bf16)]
         + [dma((5,)), dma((4,)), dma, dma, dma, dma, dma, dma((Z,)), dma, dma, dma, dma, dma]
-        + [regular((Y,)), regular((Z,))],
+        + [regular((Y,)), regular((Z,)), regular],
         compiler_params=pltpu.CompilerParams(
             collective_id=0, has_side_effects=True, vmem_limit_bytes=32 * 1024 * 1024
         ),

time: 47.2 us -> 48 us (1.017)
  Pallas kernels: 46.4 us -> 47.2 us
    pallas_call x1, Pallas kernels: 45.4 us -> 46.2 us  [shards(): pl.pallas_call(kernel, out_shape=outs, in_specs=[anywhere] * 6, out_specs...]
where the time goes in v5:
time: 48 us; the launch traced here: 47.8 us
  Pallas kernels  47.2 us (98%)
  between operations  0.64 us (1%)
    pallas_call x1, Pallas kernels, shards(): pl.pallas_call(kernel, out_shape=outs, in_specs=[anywhere] * 6, out_specs...  46.2 us
    pallas_call x1, Pallas kernels, shards(): pl.pallas_call(write_out, out_shape=outs, in_specs=[pl.BlockSpec(memory_s...  0.96 us

profile of v5, /device:TPU:1, one launch (start us, length us, event | category | flops | bytes accessed | tf_op | source)
XLA Modules:
  0.0 47.8 jit_solution(5089043943030308294)
XLA Ops:
  0.6 46.2 %shard_map.101 = (bf16[8,8,2,2,256]{4,3,2,1,0:T(2,128)(2,1)S(1)}, f32[256,256]{1,0:T(8,128)S(1)}, f32[256,256]{1,0:T(8,128)S(1)}, bf16[256,256]{1,0:T(8,128)(2,1)S(1)}, bf16[256,256]{1,0:T(8,128)(2,1)S(1)}) custom-call(s32[1,2]{1,0:T(1,128)} %refresh_ref.1, bf16[8,8,2,2,256]{4,3,2,1,0:T(2,128)(2,1)} %bitcast.12, f32[256,256]{1,0:T(8,128)} %bitcast.10, ...), custom_call_target="tpu_custom_call" | custom-call | tf_op jit(solution)/shard_map/pallas_call | solution.py:277
  46.9 1.0 %shard_map.102 = (bf16[8,8,2,2,256]{4,3,2,1,0:T(2,128)(2,1)}, f32[256,256]{1,0:T(8,128)}, f32[256,256]{1,0:T(8,128)}, bf16[256,256]{1,0:T(8,128)(2,1)}, bf16[256,256]{1,0:T(8,128)(2,1)}) custom-call(bf16[8,8,2,2,256]{4,3,2,1,0:T(2,128)(2,1)S(1)} %get-tuple-element.15.refs_0_, f32[256,256]{1,0:T(8,128)S(1)} %get-tuple-element.16.refs_1_, ...), custom_call_target="tpu_custom_call" | custom-call | tf_op jit(solution)/shard_map/pallas_call | solution.py:291

commit v6 on v5

--- a/solution.py
+++ b/solution.py
@@ -61,21 +61,27 @@
     out_ref, nl_ref, nr_ref, nlr_ref, nrr_ref,
     refresh, both, relay, block, back, both_back, ls, rs, lr, rr, nl, nr, nlr, nrr,
     load_sem, store_sem, send_core, recv_core, send_row, send_down, send_up, recv_relay, recv_block,
-    send_back, recv_back, send_out, recv_out, here_row, here_up, here_corner,
+    send_back, recv_back, send_out, recv_out, here_row, here_up, here_proxy, here_corner,
 ):
     me, own = lax.axis_index("fsdp"), lax.axis_index("own")
     y, z, c = me // (Z * C), (me // C) % Z, me % C
     ORDER = (0, 1, 2, 3, 6, 7, 4, 5)
     rank = (jnp.where(y < 4, y, (y + 2) % 4 + 4) + jnp.where(z == 0, Y - 1, 0)) % Y
+
+    chip = (y == 0) & (z == 0)
     plane = (own == 0) & (c == 0)
-    corner = plane & (y == 0) & (z == 0)
-    between = plane & (z > 0) & (z < Z - 1)
+    corner, sibling = plane & chip, (own == 0) & (c == 1) & chip
+    proxy = (own == 1) & (c == 0) & chip
+    others = plane & jnp.logical_not(chip)
+    middle = others & (z > 0) & (z < Z - 1)
+    last = (z == Z - 1).astype(jnp.int32)
+    count = lambda flag: flag.astype(jnp.int32)
 
     def ordered(r):
         return jnp.where(z == 0, ORDER[(r + 1) % Y], ORDER[r])
 
-    def at(py, pz, pc=c):
-        return ((py * Z + pz) * C + pc, own)
+    def at(py, pz, pc=c, px=own):
+        return ((py * Z + pz) * C + pc, px)
 
     def signal(sem, device):
         pl.semaphore_signal(sem, inc=1, device_id=device, device_id_type=MESH)
@@ -99,21 +105,39 @@
         lax.fori_loop(low, high, step, 0)
 
     barrier = pltpu.get_barrier_semaphore()
-    signal(barrier, at(y, z, 1 - c))
-    for r in range(1, Y):
-
-        @pl.when(r > rank)
-        def _():
-            signal(barrier, at(ordered(r), z))
-
-    @functools.partial(repeat, jnp.where(corner, Z - 1, z + 1), Z)
-    def _(pz):
+
+    @pl.when(jnp.logical_not(corner))
+    def _():
+        signal(barrier, at(y, z, 1 - c))
+        for r in range(1, Y):
+
+            @pl.when(r > rank)
+            def _():
+                signal(barrier, at(ordered(r), z))
+
+        @functools.partial(repeat, z + 1, Z)
+        def _(pz):
+            for py in range(Y):
+                signal(barrier, at(py, pz))
+
+    @pl.when(others & (z > 0))
+    def _():
+        signal(barrier, at(0, 0))
+
+    @pl.when((others & (z == 0)) | sibling)
+    def _():
+        signal(barrier, at(0, 0, 0, 1))
+
+    @pl.when(proxy)
+    def _():
+        @functools.partial(repeat, 0, Z)
+        def _(pz):
+            signal(barrier, at(0, pz, c, 0))
+
+    @pl.when(corner)
+    def _():
         for py in range(Y):
-            signal(barrier, at(py, pz))
-
-    @pl.when(between)
-    def _():
-        signal(barrier, at(0, 0))
+            signal(barrier, at(py, Z - 1))
 
     loads = [
         pltpu.make_async_copy(src, dst, load_sem.at[i])
@@ -123,90 +147,128 @@
     ]
     for copy in loads:
         copy.start()
-    greetings = 1 + rank + Y * z - between.astype(jnp.int32)
-    pl.semaphore_wait(barrier, jnp.where(corner, 1 + rank + Y * (Z - 2), greetings))
-    for r in range(Y - 1):
-
-        @pl.when(r < rank)
-        def _():
-            signal(here_row.at[rank], at(ordered(r), z))
-
-    @functools.partial(repeat, (between & (y == 0)).astype(jnp.int32), z)
-    def _(pz):
-        signal(here_up.at[z], at(y, pz))
+    greetings = 1 + rank + Y * z - count(sibling) - count(middle) + count(others & (y == 0)) + Y * count(proxy)
+    pl.semaphore_wait(barrier, jnp.where(corner, 2 + rank + Y * (Z - 1), greetings))
+
+    def gather():
+        for r in range(Y - 1):
+
+            @pl.when(r < rank)
+            def _():
+                signal(here_row.at[rank], at(ordered(r), z))
+
+        to_proxy = others & (y == 0)
+
+        @pl.when(to_proxy)
+        def _():
+            signal(here_proxy.at[z], at(0, 0, 0, 1))
+
+        @functools.partial(repeat, count(to_proxy), z)
+        def _(pz):
+            signal(here_up.at[z], at(y, pz))
+
+        @pl.when(jnp.logical_not(sibling))
+        def _():
+            remote(g_ref.at[:, :, 1 - c], both.at[:, :, c], send_core, recv_core, at(y, z, 1 - c))
+
+        @pl.when(proxy)
+        def _():
+            remote(g_ref.at[:, :, 1 - c], both.at[:, :, c], send_core, recv_core, at(y, z, 1 - c, 0))
+
+        local(g_ref.at[:, :, c], both.at[:, :, c], recv_core)
+        drained(both, recv_core)
+
+        def to_row(py, px=own):
+            remote(both.at[py, z], block.at[y, z], send_row, recv_block.at[last], at(py, z, c, px))
+
+            @functools.partial(repeat, z + 1, Z)
+            def _(pz):
+                remote(both.at[py, pz], relay.at[pz, y], send_row, recv_relay.at[pz], at(py, z, c, px))
+
+        for r in range(Y - 1):
+
+            @pl.when(r < rank)
+            def _():
+                to_row(ordered(r))
+
+        def down(py, pz):
+            remote(both.at[py, pz], block.at[y, z], send_down, recv_block.at[last], at(py, pz))
+
+        for pz in (3, 4, 0, 5, 2, 1, 6):
+
+            @pl.when(pz < z)
+            def _():
+                for py in range(Y):
+                    if py or pz:
+                        down(py, pz)
+                    else:
+                        pl.when(jnp.logical_not(middle))(functools.partial(down, 0, 0))
+
+        local(both.at[y, z], block.at[y, z], recv_block.at[last])
+
+        @functools.partial(repeat, z + 1, Z)
+        def _(pz):
+            local(both.at[y, pz], relay.at[pz, y], recv_relay.at[pz])
+
+        for r in range(1, Y):
+            awaited = r > rank
+            if r == Y - 1:
+                awaited &= jnp.logical_not(others & (z == 0))
+
+            @pl.when(awaited)
+            def _():
+                pl.semaphore_wait(here_row.at[r], 1)
+                to_row(ordered(r))
+
+        @pl.when(proxy)
+        def _():
+            for py in range(1, Y):
+                to_row(py, 0)
+
+        @functools.partial(repeat, z + 1, Z)
+        def _(pz):
+            drained(relay.at[pz], recv_relay.at[pz])
+            pl.semaphore_wait(here_up.at[pz], 1)
+            remote(relay.at[pz], block.at[:, z], send_up, recv_block.at[0], at(y, pz))
+
+            @pl.when(proxy)
+            def _():
+                pl.semaphore_wait(here_proxy.at[pz], 1)
+                remote(relay.at[pz], block.at[:, z], send_up, recv_block.at[0], at(y, pz, c, 0))
+
+        repeat(0, 1 + count(proxy) - count(sibling), lambda i: drained(both.at[:, :, 0], send_core))
+        partners = Y - 1 + (Y - 1) * count(proxy) - count(others & (z == 0))
+        repeat(0, partners * (Z - z), lambda i: drained(relay.at[0, 0], send_row))
+        repeat(0, z, lambda i: drained(relay.at[0, 1:], send_down))
+        repeat(0, z - count(middle), lambda i: drained(relay.at[0, 0], send_down))
+        repeat(0, (Z - 1 - z) * (1 + count(proxy)), lambda i: drained(relay.at[0], send_up))
+
+    pl.when(jnp.logical_not(corner))(gather)
 
     @pl.when(corner)
     def _():
-        @functools.partial(repeat, 1, Z - 1)
-        def _(pz):
-            for py in range(Y):
+        signal(here_corner, at(0, 0, 0, 1))
+        signal(here_corner, at(0, 0, 1))
+
+        @functools.partial(repeat, 0, Z)
+        def _(pz):
+            for py in range(1, Y):
                 signal(here_corner, at(py, pz))
 
-    remote(g_ref.at[:, :, 1 - c], both.at[:, :, c], send_core, recv_core, at(y, z, 1 - c))
-    local(g_ref.at[:, :, c], both.at[:, :, c], recv_core)
-    drained(both, recv_core)
-
-    def to_row(py):
-        remote(both.at[py, z], block.at[y, z], send_row, recv_block, at(py, z))
-
-        @functools.partial(repeat, z + 1, Z)
-        def _(pz):
-            remote(both.at[py, pz], relay.at[pz, y], send_row, recv_relay.at[pz], at(py, z))
-
-    for r in range(Y - 1):
-
-        @pl.when(r < rank)
-        def _():
-            to_row(ordered(r))
-
-    def down(py, pz):
-        remote(both.at[py, pz], block.at[y, z], send_down, recv_block, at(py, pz))
-
-    for pz in (3, 4, 0, 5, 2, 1, 6):
-
-        @pl.when(pz < z)
-        def _():
-            for py in range(Y):
-                if py or pz:
-                    down(py, pz)
-                else:
-                    pl.when(jnp.logical_not(between))(functools.partial(down, 0, 0))
-
-    local(both.at[y, z], block.at[y, z], recv_block)
-
-    @functools.partial(repeat, z + 1, Z)
-    def _(pz):
-        local(both.at[y, pz], relay.at[pz, y], recv_relay.at[pz])
-
-    for r in range(1, Y):
-
-        @pl.when(r > rank)
-        def _():
-            pl.semaphore_wait(here_row.at[r], 1)
-            to_row(ordered(r))
-
-    @pl.when(between)
-    def _():
-        pl.semaphore_wait(here_corner, 1)
-        down(0, 0)
-
-    @functools.partial(repeat, z + 1, Z)
-    def _(pz):
-        drained(relay.at[pz], recv_relay.at[pz])
-
-        @pl.when(jnp.logical_not(corner) | (pz == Z - 1))
-        def _():
-            pl.semaphore_wait(here_up.at[pz], 1)
-
-        remote(relay.at[pz], block.at[:, z], send_up, recv_block, at(y, pz))
-
-    drained(both.at[:, :, 0], send_core)
-    repeat(z, Z, lambda i: drained(relay.at[0, 1:], send_row))
-    repeat(0, z, lambda i: drained(relay.at[0], send_down))
-    repeat(z + 1, Z, lambda i: drained(relay.at[0], send_up))
+            @pl.when(pz > 0)
+            def _():
+                signal(here_corner, at(0, pz))
+
     for copy in loads:
         copy.wait()
-    drained(block, recv_block)
+    drained(block.at[:, : Z - 1], recv_block.at[0])
+
+    @pl.when(proxy)
+    def _():
+        pl.semaphore_wait(here_corner, 1)
+        remote(block.at[:, : Z - 1], block.at[:, : Z - 1], send_up, recv_block.at[0], at(0, 0, 0, 0))
+
+    drained(block.at[:, Z - 1], recv_block.at[1])
 
     g = block[...].reshape(B, B)
     new_left = decay_rate * ls[...] + (1.0 - decay_rate) * dot(g, g, ((1,), (1,)))
@@ -233,6 +295,10 @@
     grafted = (preconditioned * (grad_norm / norm)).astype(bf16)
     back[...] = grafted.reshape(Y, Z, C, 2, B)
 
+    @pl.when(others | sibling)
+    def _():
+        pl.semaphore_wait(here_corner, 1)
+
     remote(back.at[:, :, 1 - c], both_back.at[:, :, c], send_back, recv_back, at(y, z, 1 - c))
     local(back.at[:, :, c], both_back.at[:, :, c], recv_back)
     drained(both_back, recv_back)
@@ -251,6 +317,11 @@
     drained(both_back.at[:, :, 0], send_back)
     for copy in stores:
         copy.wait()
+
+    @pl.when(proxy)
+    def _():
+        drained(block.at[:, 1:], send_up)
+
     drained(out_ref, recv_out)
     drained(both_back.at[1:], send_out)
     drained(both_back.at[0, 1:], send_out)
@@ -282,8 +353,8 @@
         scratch_shapes=[pltpu.SMEM((1, 2), jnp.int32)]
         + [pltpu.VMEM(r, bf16) for r in (rows, (Z, Y, C, 2, B), rows, rows, rows)]
         + [pltpu.VMEM((B, B), t) for t in (f32, f32, bf16, bf16, f32, f32, bf16, bf16)]
-        + [dma((5,)), dma((4,)), dma, dma, dma, dma, dma, dma((Z,)), dma, dma, dma, dma, dma]
-        + [regular((Y,)), regular((Z,)), regular],
+        + [dma((5,)), dma((4,)), dma, dma, dma, dma, dma, dma((Z,)), dma((2,)), dma, dma, dma, dma]
+        + [regular((Y,)), regular((Z,)), regular((Z,)), regular],
         compiler_params=pltpu.CompilerParams(
             collective_id=0, has_side_effects=True, vmem_limit_bytes=32 * 1024 * 1024
         ),

time: 48 us -> 42.4 us (0.88)
  Pallas kernels: 47.2 us -> 41.6 us
    pallas_call x1, Pallas kernels: 46.2 us -> 40.6 us  [shards(): pl.pallas_call(kernel, out_shape=outs, in_specs=[anywhere] * 6, out_specs...]
where the time goes in v6:
time: 42.4 us; the launch traced here: 42.2 us
  Pallas kernels  41.6 us (98%)
  between operations  0.64 us (2%)
    pallas_call x1, Pallas kernels, shards(): pl.pallas_call(kernel, out_shape=outs, in_specs=[anywhere] * 6, out_specs...  40.6 us
    pallas_call x1, Pallas kernels, shards(): pl.pallas_call(write_out, out_shape=outs, in_specs=[pl.BlockSpec(memory_s...  0.96 us

profile of v6, /device:TPU:1, one launch (start us, length us, event | category | flops | bytes accessed | tf_op | source)
XLA Modules:
  0.0 42.2 jit_solution(3321640875453449549)
XLA Ops:
  0.6 40.6 %shard_map.101 = (bf16[8,8,2,2,256]{4,3,2,1,0:T(2,128)(2,1)S(1)}, f32[256,256]{1,0:T(8,128)S(1)}, f32[256,256]{1,0:T(8,128)S(1)}, bf16[256,256]{1,0:T(8,128)(2,1)S(1)}, bf16[256,256]{1,0:T(8,128)(2,1)S(1)}) custom-call(s32[1,2]{1,0:T(1,128)} %refresh_ref.1, bf16[8,8,2,2,256]{4,3,2,1,0:T(2,128)(2,1)} %bitcast.12, f32[256,256]{1,0:T(8,128)} %bitcast.10, ...), custom_call_target="tpu_custom_call" | custom-call | tf_op jit(solution)/shard_map/pallas_call | solution.py:348
  41.3 1.0 %shard_map.102 = (bf16[8,8,2,2,256]{4,3,2,1,0:T(2,128)(2,1)}, f32[256,256]{1,0:T(8,128)}, f32[256,256]{1,0:T(8,128)}, bf16[256,256]{1,0:T(8,128)(2,1)}, bf16[256,256]{1,0:T(8,128)(2,1)}) custom-call(bf16[8,8,2,2,256]{4,3,2,1,0:T(2,128)(2,1)S(1)} %get-tuple-element.15.refs_0_, f32[256,256]{1,0:T(8,128)S(1)} %get-tuple-element.16.refs_1_, ...), custom_call_target="tpu_custom_call" | custom-call | tf_op jit(solution)/shard_map/pallas_call | solution.py:362

commit v7 on v6

--- a/solution.py
+++ b/solution.py
@@ -145,12 +145,19 @@
             ((refresh_ref, refresh), (ls_ref, ls), (rs_ref, rs), (lr_ref, lr), (rr_ref, rr))
         )
     ]
-    for copy in loads:
-        copy.start()
     greetings = 1 + rank + Y * z - count(sibling) - count(middle) + count(others & (y == 0)) + Y * count(proxy)
     pl.semaphore_wait(barrier, jnp.where(corner, 2 + rank + Y * (Z - 1), greetings))
 
-    def gather():
+    def announce():
+        @pl.when(jnp.logical_not(sibling))
+        def _():
+            remote(g_ref.at[:, :, 1 - c], both.at[:, :, c], send_core, recv_core, at(y, z, 1 - c))
+
+        @pl.when(proxy)
+        def _():
+            remote(g_ref.at[:, :, 1 - c], both.at[:, :, c], send_core, recv_core, at(y, z, 1 - c, 0))
+
+        local(g_ref.at[:, :, c], both.at[:, :, c], recv_core)
         for r in range(Y - 1):
 
             @pl.when(r < rank)
@@ -167,15 +174,11 @@
         def _(pz):
             signal(here_up.at[z], at(y, pz))
 
-        @pl.when(jnp.logical_not(sibling))
-        def _():
-            remote(g_ref.at[:, :, 1 - c], both.at[:, :, c], send_core, recv_core, at(y, z, 1 - c))
-
-        @pl.when(proxy)
-        def _():
-            remote(g_ref.at[:, :, 1 - c], both.at[:, :, c], send_core, recv_core, at(y, z, 1 - c, 0))
-
-        local(g_ref.at[:, :, c], both.at[:, :, c], recv_core)
+    pl.when(jnp.logical_not(corner))(announce)
+    for copy in loads:
+        copy.start()
+
+    def gather():
         drained(both, recv_core)
 
         def to_row(py, px=own):
@@ -194,9 +197,8 @@
         def down(py, pz):
             remote(both.at[py, pz], block.at[y, z], send_down, recv_block.at[last], at(py, pz))
 
-        for pz in (3, 4, 0, 5, 2, 1, 6):
-
-            @pl.when(pz < z)
+        def down_to(pz, wanted):
+            @pl.when(wanted & (pz < z))
             def _():
                 for py in range(Y):
                     if py or pz:
@@ -204,6 +206,9 @@
                     else:
                         pl.when(jnp.logical_not(middle))(functools.partial(down, 0, 0))
 
+        for pz in (3, 4, 0):
+            down_to(pz, z == Z - 1)
+
         local(both.at[y, z], block.at[y, z], recv_block.at[last])
 
         @functools.partial(repeat, z + 1, Z)
@@ -219,6 +224,11 @@
             def _():
                 pl.semaphore_wait(here_row.at[r], 1)
                 to_row(ordered(r))
+
+        for pz in (3, 4, 0):
+            down_to(pz, z < Z - 1)
+        for pz in (5, 2, 1, 6):
+            down_to(pz, True)
 
         @pl.when(proxy)
         def _():
@@ -305,13 +315,11 @@
 
     @functools.partial(repeat, 0, Z)
     def _(pz):
-        for i in (4, 3, 5, 2, 6, 1, 7):
-            py = (y + i) % Y
-            remote(both_back.at[py, pz], out_ref.at[y, z], send_out, recv_out, at(py, pz))
-
-        @pl.when(pz != z)
-        def _():
-            remote(both_back.at[y, pz], out_ref.at[y, z], send_out, recv_out, at(y, pz))
+        for py in ORDER:
+
+            @pl.when((pz != z) | (py != y))
+            def _():
+                remote(both_back.at[py, pz], out_ref.at[y, z], send_out, recv_out, at(py, pz))
 
     local(both_back.at[y, z], out_ref.at[y, z], recv_out)
     drained(both_back.at[:, :, 0], send_back)

time: 42.4 us -> 42.5 us (level)
  no operation moved by 1% of the time
where the time goes in v7:
time: 42.5 us; the launch traced here: 42.3 us
  Pallas kernels  41.7 us (98%)
  between operations  0.64 us (2%)
    pallas_call x1, Pallas kernels, shards(): pl.pallas_call(kernel, out_shape=outs, in_specs=[anywhere] * 6, out_specs...  40.7 us
    pallas_call x1, Pallas kernels, shards(): pl.pallas_call(write_out, out_shape=outs, in_specs=[pl.BlockSpec(memory_s...  0.96 us

profile of v7, /device:TPU:1, one launch (start us, length us, event | category | flops | bytes accessed | tf_op | source)
XLA Modules:
  0.0 42.3 jit_solution(17320330135342786893)
XLA Ops:
  0.6 40.7 %shard_map.101 = (bf16[8,8,2,2,256]{4,3,2,1,0:T(2,128)(2,1)S(1)}, f32[256,256]{1,0:T(8,128)S(1)}, f32[256,256]{1,0:T(8,128)S(1)}, bf16[256,256]{1,0:T(8,128)(2,1)S(1)}, bf16[256,256]{1,0:T(8,128)(2,1)S(1)}) custom-call(s32[1,2]{1,0:T(1,128)} %refresh_ref.1, bf16[8,8,2,2,256]{4,3,2,1,0:T(2,128)(2,1)} %bitcast.12, f32[256,256]{1,0:T(8,128)} %bitcast.10, ...), custom_call_target="tpu_custom_call" | custom-call | tf_op jit(solution)/shard_map/pallas_call | solution.py:356
  41.4 1.0 %shard_map.102 = (bf16[8,8,2,2,256]{4,3,2,1,0:T(2,128)(2,1)}, f32[256,256]{1,0:T(8,128)}, f32[256,256]{1,0:T(8,128)}, bf16[256,256]{1,0:T(8,128)(2,1)}, bf16[256,256]{1,0:T(8,128)(2,1)}) custom-call(bf16[8,8,2,2,256]{4,3,2,1,0:T(2,128)(2,1)S(1)} %get-tuple-element.15.refs_0_, f32[256,256]{1,0:T(8,128)S(1)} %get-tuple-element.16.refs_1_, ...), custom_call_target="tpu_custom_call" | custom-call | tf_op jit(solution)/shard_map/pallas_call | solution.py:370

commit v8 on v7

--- a/solution.py
+++ b/solution.py
@@ -59,7 +59,7 @@
 def kernel(
     refresh_ref, g_ref, ls_ref, rs_ref, lr_ref, rr_ref,
     out_ref, nl_ref, nr_ref, nlr_ref, nrr_ref,
-    refresh, both, relay, block, back, both_back, ls, rs, lr, rr, nl, nr, nlr, nrr,
+    refresh, mine, both, relay, block, back, both_back, ls, rs, lr, rr, nl, nr, nlr, nrr,
     load_sem, store_sem, send_core, recv_core, send_row, send_down, send_up, recv_relay, recv_block,
     send_back, recv_back, send_out, recv_out, here_row, here_up, here_proxy, here_corner,
 ):
@@ -104,6 +104,9 @@
 
         lax.fori_loop(low, high, step, 0)
 
+    fetch = pltpu.make_async_copy(g_ref, mine, load_sem.at[5])
+    fetch.start()
+
     barrier = pltpu.get_barrier_semaphore()
 
     @pl.when(jnp.logical_not(corner))
@@ -149,15 +152,6 @@
     pl.semaphore_wait(barrier, jnp.where(corner, 2 + rank + Y * (Z - 1), greetings))
 
     def announce():
-        @pl.when(jnp.logical_not(sibling))
-        def _():
-            remote(g_ref.at[:, :, 1 - c], both.at[:, :, c], send_core, recv_core, at(y, z, 1 - c))
-
-        @pl.when(proxy)
-        def _():
-            remote(g_ref.at[:, :, 1 - c], both.at[:, :, c], send_core, recv_core, at(y, z, 1 - c, 0))
-
-        local(g_ref.at[:, :, c], both.at[:, :, c], recv_core)
         for r in range(Y - 1):
 
             @pl.when(r < rank)
@@ -174,7 +168,20 @@
         def _(pz):
             signal(here_up.at[z], at(y, pz))
 
+        fetch.wait()
+
+        @pl.when(jnp.logical_not(sibling))
+        def _():
+            remote(mine.at[:, 1 - c], both.at[:, c], send_core, recv_core, at(y, z, 1 - c))
+
+        @pl.when(proxy)
+        def _():
+            remote(mine.at[:, 1 - c], both.at[:, c], send_core, recv_core, at(y, z, 1 - c, 0))
+
+        local(mine.at[:, c], both.at[:, c], recv_core)
+
     pl.when(jnp.logical_not(corner))(announce)
+    pl.when(corner)(fetch.wait)
     for copy in loads:
         copy.start()
 
@@ -182,11 +189,11 @@
         drained(both, recv_core)
 
         def to_row(py, px=own):
-            remote(both.at[py, z], block.at[y, z], send_row, recv_block.at[last], at(py, z, c, px))
+            remote(both.at[py * Z + z], block.at[y, z], send_row, recv_block.at[last], at(py, z, c, px))
 
             @functools.partial(repeat, z + 1, Z)
             def _(pz):
-                remote(both.at[py, pz], relay.at[pz, y], send_row, recv_relay.at[pz], at(py, z, c, px))
+                remote(both.at[py * Z + pz], relay.at[pz, y], send_row, recv_relay.at[pz], at(py, z, c, px))
 
         for r in range(Y - 1):
 
@@ -195,7 +202,7 @@
                 to_row(ordered(r))
 
         def down(py, pz):
-            remote(both.at[py, pz], block.at[y, z], send_down, recv_block.at[last], at(py, pz))
+            remote(both.at[py * Z + pz], block.at[y, z], send_down, recv_block.at[last], at(py, pz))
 
         def down_to(pz, wanted):
             @pl.when(wanted & (pz < z))
@@ -209,11 +216,11 @@
         for pz in (3, 4, 0):
             down_to(pz, z == Z - 1)
 
-        local(both.at[y, z], block.at[y, z], recv_block.at[last])
+        local(both.at[y * Z + z], block.at[y, z], recv_block.at[last])
 
         @functools.partial(repeat, z + 1, Z)
         def _(pz):
-            local(both.at[y, pz], relay.at[pz, y], recv_relay.at[pz])
+            local(both.at[y * Z + pz], relay.at[pz, y], recv_relay.at[pz])
 
         for r in range(1, Y):
             awaited = r > rank
@@ -246,7 +253,7 @@
                 pl.semaphore_wait(here_proxy.at[pz], 1)
                 remote(relay.at[pz], block.at[:, z], send_up, recv_block.at[0], at(y, pz, c, 0))
 
-        repeat(0, 1 + count(proxy) - count(sibling), lambda i: drained(both.at[:, :, 0], send_core))
+        repeat(0, 1 + count(proxy) - count(sibling), lambda i: drained(both.at[:, 0], send_core))
         partners = Y - 1 + (Y - 1) * count(proxy) - count(others & (z == 0))
         repeat(0, partners * (Z - z), lambda i: drained(relay.at[0, 0], send_row))
         repeat(0, z, lambda i: drained(relay.at[0, 1:], send_down))
@@ -303,14 +310,14 @@
     grad_norm = jnp.sqrt(jnp.sum(wide * wide, keepdims=True))
     norm = jnp.sqrt(jnp.sum(preconditioned * preconditioned, keepdims=True) + epsilon)
     grafted = (preconditioned * (grad_norm / norm)).astype(bf16)
-    back[...] = grafted.reshape(Y, Z, C, 2, B)
+    back[...] = grafted.reshape(Y * Z, C, 2, B)
 
     @pl.when(others | sibling)
     def _():
         pl.semaphore_wait(here_corner, 1)
 
-    remote(back.at[:, :, 1 - c], both_back.at[:, :, c], send_back, recv_back, at(y, z, 1 - c))
-    local(back.at[:, :, c], both_back.at[:, :, c], recv_back)
+    remote(back.at[:, 1 - c], both_back.at[:, c], send_back, recv_back, at(y, z, 1 - c))
+    local(back.at[:, c], both_back.at[:, c], recv_back)
     drained(both_back, recv_back)
 
     @functools.partial(repeat, 0, Z)
@@ -319,10 +326,10 @@
 
             @pl.when((pz != z) | (py != y))
             def _():
-                remote(both_back.at[py, pz], out_ref.at[y, z], send_out, recv_out, at(py, pz))
-
-    local(both_back.at[y, z], out_ref.at[y, z], recv_out)
-    drained(both_back.at[:, :, 0], send_back)
+                remote(both_back.at[py * Z + pz], out_ref.at[y, z], send_out, recv_out, at(py, pz))
+
+    local(both_back.at[y * Z + z], out_ref.at[y, z], recv_out)
+    drained(both_back.at[:, 0], send_back)
     for copy in stores:
         copy.wait()
 
@@ -332,7 +339,6 @@
 
     drained(out_ref, recv_out)
     drained(both_back.at[1:], send_out)
-    drained(both_back.at[0, 1:], send_out)
 
 
 def write_out(*refs):
@@ -347,11 +353,11 @@
 def shards(gradient, refresh, left_stat, right_stat, left_root, right_root):
     anywhere = pl.BlockSpec(memory_space=pl.ANY)
     square = lambda dtype: jax.ShapeDtypeStruct((B, B), dtype)
-    rows = (Y, Z, C, 2, B)
+    rows, flat = (Y, Z, C, 2, B), (Y * Z, C, 2, B)
     outs = (jax.ShapeDtypeStruct(rows, bf16), square(f32), square(f32), square(bf16), square(bf16))
     dma, regular = pltpu.SemaphoreType.DMA, pltpu.SemaphoreType.REGULAR
     operands = (
-        refresh, gradient.reshape(rows), left_stat[0], right_stat[0], left_root[0], right_root[0]
+        refresh, gradient.reshape(flat), left_stat[0], right_stat[0], left_root[0], right_root[0]
     )
     results = pl.pallas_call(
         kernel,
@@ -359,9 +365,9 @@
         in_specs=[anywhere] * 6,
         out_specs=(anywhere,) * 5,
         scratch_shapes=[pltpu.SMEM((1, 2), jnp.int32)]
-        + [pltpu.VMEM(r, bf16) for r in (rows, (Z, Y, C, 2, B), rows, rows, rows)]
+        + [pltpu.VMEM(r, bf16) for r in (flat, flat, (Z, Y, C, 2, B), rows, flat, flat)]
         + [pltpu.VMEM((B, B), t) for t in (f32, f32, bf16, bf16, f32, f32, bf16, bf16)]
-        + [dma((5,)), dma((4,)), dma, dma, dma, dma, dma, dma((Z,)), dma((2,)), dma, dma, dma, dma]
+        + [dma((6,)), dma((4,)), dma, dma, dma, dma, dma, dma((Z,)), dma((2,)), dma, dma, dma, dma]
         + [regular((Y,)), regular((Z,)), regular((Z,)), regular],
         compiler_params=pltpu.CompilerParams(
             collective_id=0, has_side_effects=True, vmem_limit_bytes=32 * 1024 * 1024

time: 42.5 us -> 42.3 us (level)
  no operation moved by 1% of the time
where the time goes in v8:
time: 42.3 us; the launch traced here: 42.2 us
  Pallas kernels  41.5 us (98%)
  between operations  0.64 us (2%)
    pallas_call x1, Pallas kernels, shards(): pl.pallas_call(kernel, out_shape=outs, in_specs=[anywhere] * 6, out_specs...  40.6 us
    pallas_call x1, Pallas kernels, shards(): pl.pallas_call(write_out, out_shape=outs, in_specs=[pl.BlockSpec(memory_s...  0.96 us

profile of v8, /device:TPU:1, one launch (start us, length us, event | category | flops | bytes accessed | tf_op | source)
XLA Modules:
  0.0 42.2 jit_solution(18326960620671154704)
XLA Ops:
  0.6 40.6 %shard_map.101 = (bf16[8,8,2,2,256]{4,3,2,1,0:T(2,128)(2,1)S(1)}, f32[256,256]{1,0:T(8,128)S(1)}, f32[256,256]{1,0:T(8,128)S(1)}, bf16[256,256]{1,0:T(8,128)(2,1)S(1)}, bf16[256,256]{1,0:T(8,128)(2,1)S(1)}) custom-call(s32[1,2]{1,0:T(1,128)} %refresh_ref.1, bf16[64,2,2,256]{3,2,1,0:T(2,128)(2,1)} %bitcast.12, f32[256,256]{1,0:T(8,128)} %bitcast.10, ...), custom_call_target="tpu_custom_call" | custom-call | tf_op jit(solution)/shard_map/pallas_call | solution.py:362
  41.2 1.0 %shard_map.102 = (bf16[8,8,2,2,256]{4,3,2,1,0:T(2,128)(2,1)}, f32[256,256]{1,0:T(8,128)}, f32[256,256]{1,0:T(8,128)}, bf16[256,256]{1,0:T(8,128)(2,1)}, bf16[256,256]{1,0:T(8,128)(2,1)}) custom-call(bf16[8,8,2,2,256]{4,3,2,1,0:T(2,128)(2,1)S(1)} %get-tuple-element.15.refs_0_, f32[256,256]{1,0:T(8,128)S(1)} %get-tuple-element.16.refs_1_, ...), custom_call_target="tpu_custom_call" | custom-call | tf_op jit(solution)/shard_map/pallas_call | solution.py:376

commit v9 on v8

--- a/solution.py
+++ b/solution.py
@@ -65,8 +65,8 @@
 ):
     me, own = lax.axis_index("fsdp"), lax.axis_index("own")
     y, z, c = me // (Z * C), (me // C) % Z, me % C
-    ORDER = (0, 1, 2, 3, 6, 7, 4, 5)
-    rank = (jnp.where(y < 4, y, (y + 2) % 4 + 4) + jnp.where(z == 0, Y - 1, 0)) % Y
+    shift = jnp.where(z == 0, 1, 0)
+    rank = (jnp.where(y < 4, y, 11 - y) + Y - shift) % Y
 
     chip = (y == 0) & (z == 0)
     plane = (own == 0) & (c == 0)
@@ -78,7 +78,8 @@
     count = lambda flag: flag.astype(jnp.int32)
 
     def ordered(r):
-        return jnp.where(z == 0, ORDER[(r + 1) % Y], ORDER[r])
+        place = (r + shift) & (Y - 1)
+        return jnp.where(place < 4, place, 11 - place)
 
     def at(py, pz, pc=c, px=own):
         return ((py * Z + pz) * C + pc, px)
@@ -112,11 +113,7 @@
     @pl.when(jnp.logical_not(corner))
     def _():
         signal(barrier, at(y, z, 1 - c))
-        for r in range(1, Y):
-
-            @pl.when(r > rank)
-            def _():
-                signal(barrier, at(ordered(r), z))
+        repeat(rank + 1, Y, lambda r: signal(barrier, at(ordered(r), z)))
 
         @functools.partial(repeat, z + 1, Z)
         def _(pz):
@@ -152,11 +149,19 @@
     pl.semaphore_wait(barrier, jnp.where(corner, 2 + rank + Y * (Z - 1), greetings))
 
     def announce():
-        for r in range(Y - 1):
-
-            @pl.when(r < rank)
-            def _():
-                signal(here_row.at[rank], at(ordered(r), z))
+        fetch.wait()
+
+        @pl.when(jnp.logical_not(sibling))
+        def _():
+            remote(mine.at[:, 1 - c], both.at[:, c], send_core, recv_core, at(y, z, 1 - c))
+
+        @pl.when(proxy)
+        def _():
+            remote(mine.at[:, 1 - c], both.at[:, c], send_core, recv_core, at(y, z, 1 - c, 0))
+
+        local(mine.at[:, c], both.at[:, c], recv_core)
+
+        repeat(0, rank, lambda r: signal(here_row.at[rank], at(ordered(r), z)))
 
         to_proxy = others & (y == 0)
 
@@ -167,18 +172,6 @@
         @functools.partial(repeat, count(to_proxy), z)
         def _(pz):
             signal(here_up.at[z], at(y, pz))
-
-        fetch.wait()
-
-        @pl.when(jnp.logical_not(sibling))
-        def _():
-            remote(mine.at[:, 1 - c], both.at[:, c], send_core, recv_core, at(y, z, 1 - c))
-
-        @pl.when(proxy)
-        def _():
-            remote(mine.at[:, 1 - c], both.at[:, c], send_core, recv_core, at(y, z, 1 - c, 0))
-
-        local(mine.at[:, c], both.at[:, c], recv_core)
 
     pl.when(jnp.logical_not(corner))(announce)
     pl.when(corner)(fetch.wait)
@@ -195,26 +188,18 @@
             def _(pz):
                 remote(both.at[py * Z + pz], relay.at[pz, y], send_row, recv_relay.at[pz], at(py, z, c, px))
 
-        for r in range(Y - 1):
-
-            @pl.when(r < rank)
-            def _():
-                to_row(ordered(r))
-
-        def down(py, pz):
-            remote(both.at[py * Z + pz], block.at[y, z], send_down, recv_block.at[last], at(py, pz))
-
-        def down_to(pz, wanted):
-            @pl.when(wanted & (pz < z))
-            def _():
-                for py in range(Y):
-                    if py or pz:
-                        down(py, pz)
-                    else:
-                        pl.when(jnp.logical_not(middle))(functools.partial(down, 0, 0))
-
-        for pz in (3, 4, 0):
-            down_to(pz, z == Z - 1)
+        repeat(0, rank, lambda r: to_row(ordered(r)))
+
+        def down_to(pz):
+            def down(py):
+                remote(both.at[py * Z + pz], block.at[y, z], send_down, recv_block.at[last], at(py, pz))
+
+            repeat(count(middle & (pz == 0)), Y, down)
+
+        @pl.when(z == Z - 1)
+        def _():
+            for pz in (3, 4, 0):
+                down_to(pz)
 
         local(both.at[y * Z + z], block.at[y, z], recv_block.at[last])
 
@@ -222,25 +207,23 @@
         def _(pz):
             local(both.at[y * Z + pz], relay.at[pz, y], recv_relay.at[pz])
 
-        for r in range(1, Y):
-            awaited = r > rank
-            if r == Y - 1:
-                awaited &= jnp.logical_not(others & (z == 0))
-
-            @pl.when(awaited)
-            def _():
-                pl.semaphore_wait(here_row.at[r], 1)
-                to_row(ordered(r))
-
-        for pz in (3, 4, 0):
-            down_to(pz, z < Z - 1)
-        for pz in (5, 2, 1, 6):
-            down_to(pz, True)
+        @functools.partial(repeat, rank + 1, Y - count(others & (z == 0)))
+        def _(r):
+            pl.semaphore_wait(here_row.at[r], 1)
+            to_row(ordered(r))
+
+        @pl.when(z == Z - 1)
+        def _():
+            for pz in (5, 2, 1, 6):
+                down_to(pz)
+
+        @pl.when(z < Z - 1)
+        def _():
+            repeat(0, z, down_to)
 
         @pl.when(proxy)
         def _():
-            for py in range(1, Y):
-                to_row(py, 0)
+            repeat(1, Y, lambda py: to_row(py, 0))
 
         @functools.partial(repeat, z + 1, Z)
         def _(pz):
@@ -322,8 +305,8 @@
 
     @functools.partial(repeat, 0, Z)
     def _(pz):
-        for py in ORDER:
-
+        @functools.partial(repeat, 0, Y)
+        def _(py):
             @pl.when((pz != z) | (py != y))
             def _():
                 remote(both_back.at[py * Z + pz], out_ref.at[y, z], send_out, recv_out, at(py, pz))

time: 42.3 us -> 42.4 us (level)
  no operation moved by 1% of the time
where the time goes in v9:
time: 42.4 us; the launch traced here: 42.3 us
  Pallas kernels  41.6 us (98%)
  between operations  0.64 us (2%)
    pallas_call x1, Pallas kernels, shards(): pl.pallas_call(kernel, out_shape=outs, in_specs=[anywhere] * 6, out_specs...  40.7 us
    pallas_call x1, Pallas kernels, shards(): pl.pallas_call(write_out, out_shape=outs, in_specs=[pl.BlockSpec(memory_s...  0.96 us

profile of v9, /device:TPU:1, one launch (start us, length us, event | category | flops | bytes accessed | tf_op | source)
XLA Modules:
  0.0 42.3 jit_solution(1643399593569966473)
XLA Ops:
  0.6 40.7 %shard_map.101 = (bf16[8,8,2,2,256]{4,3,2,1,0:T(2,128)(2,1)S(1)}, f32[256,256]{1,0:T(8,128)S(1)}, f32[256,256]{1,0:T(8,128)S(1)}, bf16[256,256]{1,0:T(8,128)(2,1)S(1)}, bf16[256,256]{1,0:T(8,128)(2,1)S(1)}) custom-call(s32[1,2]{1,0:T(1,128)} %refresh_ref.1, bf16[64,2,2,256]{3,2,1,0:T(2,128)(2,1)} %bitcast.12, f32[256,256]{1,0:T(8,128)} %bitcast.10, ...), custom_call_target="tpu_custom_call" | custom-call | tf_op jit(solution)/shard_map/pallas_call | solution.py:345
  41.3 1.0 %shard_map.102 = (bf16[8,8,2,2,256]{4,3,2,1,0:T(2,128)(2,1)}, f32[256,256]{1,0:T(8,128)}, f32[256,256]{1,0:T(8,128)}, bf16[256,256]{1,0:T(8,128)(2,1)}, bf16[256,256]{1,0:T(8,128)(2,1)}) custom-call(bf16[8,8,2,2,256]{4,3,2,1,0:T(2,128)(2,1)S(1)} %get-tuple-element.15.refs_0_, f32[256,256]{1,0:T(8,128)S(1)} %get-tuple-element.16.refs_1_, ...), custom_call_target="tpu_custom_call" | custom-call | tf_op jit(solution)/shard_map/pallas_call | solution.py:359

commit v10 on v9

--- a/solution.py
+++ b/solution.py
@@ -20,16 +20,6 @@
 
 def dot(a, b, dims=((1,), (0,))):
     return lax.dot_general(a, b, (dims, ((), ())), preferred_element_type=f32)
-
-
-def split(a, wide):
-    high = a.astype(bf16)
-    return (high, (a - high.astype(f32)).astype(bf16)) if wide else (high,)
-
-
-def product(a, b):
-    high = dot(a[0], b[0])
-    return high if len(a) == 1 else high + (dot(a[0], b[1]) + dot(a[1], b[0]))
 
 
 def inverse_fourth_roots(stats):
@@ -40,18 +30,17 @@
     m = [stats[i] * (0.25 / frobenius[i]) for i in n]
     root = None
     for sweep in range(ITERS):
-        wide = sweep >= ITERS - 2
-        parts = [split(x, wide) for x in m]
+        low = [x.astype(bf16) for x in m]
         if sweep < ITERS - 1:
-            r = [dot(parts[i][0], parts[i][0]) - 2.5 * m[i] for i in n]
+            r = [dot(low[i], low[i]) - 2.5 * m[i] for i in n]
         if root is None:
             root = [jnp.where(on_diagonal, 1.25, 0.0) - x for x in m]
         else:
-            root = [1.25 * root[i] - product(split(root[i], wide), parts[i]) for i in n]
+            root = [1.25 * root[i] - dot(root[i].astype(bf16), low[i]) for i in n]
         if sweep < ITERS - 1:
-            high = [x.astype(bf16) for x in r]
-            r4 = [3.125 * r[i] + dot(high[i], high[i]) for i in n]
-            m = [2.44140625 * m[i] + product(split(r4[i], wide), parts[i]) for i in n]
+            r_low = [x.astype(bf16) for x in r]
+            r4 = [3.125 * r[i] + dot(r_low[i], r_low[i]) for i in n]
+            m = [2.44140625 * m[i] + dot(r4[i].astype(bf16), low[i]) for i in n]
     scale = [jnp.exp(-0.25 * jnp.log(c)) for c in frobenius]
     return [root[i] * scale[i] for i in n]
 
@@ -61,7 +50,7 @@
     out_ref, nl_ref, nr_ref, nlr_ref, nrr_ref,
     refresh, mine, both, relay, block, back, both_back, ls, rs, lr, rr, nl, nr, nlr, nrr,
     load_sem, store_sem, send_core, recv_core, send_row, send_down, send_up, recv_relay, recv_block,
-    send_back, recv_back, send_out, recv_out, here_row, here_up, here_proxy, here_corner,
+    send_back, recv_back, send_first, send_out, recv_out, here_row, here_up, here_proxy, here_corner,
 ):
     me, own = lax.axis_index("fsdp"), lax.axis_index("own")
     y, z, c = me // (Z * C), (me // C) % Z, me % C
@@ -190,16 +179,16 @@
 
         repeat(0, rank, lambda r: to_row(ordered(r)))
 
+        def down(py, pz):
+            remote(both.at[py * Z + pz], block.at[y, z], send_down, recv_block.at[last], at(py, pz))
+
         def down_to(pz):
-            def down(py):
-                remote(both.at[py * Z + pz], block.at[y, z], send_down, recv_block.at[last], at(py, pz))
-
-            repeat(count(middle & (pz == 0)), Y, down)
+            repeat(count(middle & (pz == 0)), Y, lambda py: down(py, pz))
 
         @pl.when(z == Z - 1)
         def _():
             for pz in (3, 4, 0):
-                down_to(pz)
+                repeat(3, 3 + Y, lambda i, pz=pz: down(i & (Y - 1), pz))
 
         local(both.at[y * Z + z], block.at[y, z], recv_block.at[last])
 
@@ -215,7 +204,7 @@
         @pl.when(z == Z - 1)
         def _():
             for pz in (5, 2, 1, 6):
-                down_to(pz)
+                repeat(3, 3 + Y, lambda i, pz=pz: down(i & (Y - 1), pz))
 
         @pl.when(z < Z - 1)
         def _():
@@ -299,6 +288,21 @@
     def _():
         pl.semaphore_wait(here_corner, 1)
 
+    for py in range(2):
+        for pc in range(C):
+            here = (z == 0) & (y == py) & (c == pc)
+            served = (own != 0) if py == 0 and pc == 0 else own >= 0
+
+            @pl.when(served & jnp.logical_not(here))
+            def _():
+                remote(back.at[py * Z, pc], out_ref.at[y, z, c], send_first, recv_out, at(py, 0, pc))
+
+            @pl.when(served & here)
+            def _():
+                local(back.at[py * Z, pc], out_ref.at[y, z, c], recv_out)
+
+    first = (z == 0) & (y < 2) & jnp.logical_not(corner)
+
     remote(back.at[:, 1 - c], both_back.at[:, c], send_back, recv_back, at(y, z, 1 - c))
     local(back.at[:, c], both_back.at[:, c], recv_back)
     drained(both_back, recv_back)
@@ -307,11 +311,14 @@
     def _(pz):
         @functools.partial(repeat, 0, Y)
         def _(py):
-            @pl.when((pz != z) | (py != y))
+            @pl.when(((pz != z) | (py != y)) & ((pz > 0) | (py > 1) | (plane & (py == 0))))
             def _():
                 remote(both_back.at[py * Z + pz], out_ref.at[y, z], send_out, recv_out, at(py, pz))
 
-    local(both_back.at[y * Z + z], out_ref.at[y, z], recv_out)
+    @pl.when(jnp.logical_not(first))
+    def _():
+        local(both_back.at[y * Z + z], out_ref.at[y, z], recv_out)
+
     drained(both_back.at[:, 0], send_back)
     for copy in stores:
         copy.wait()
@@ -321,7 +328,9 @@
         drained(block.at[:, 1:], send_up)
 
     drained(out_ref, recv_out)
-    drained(both_back.at[1:], send_out)
+    drained(both_back.at[4:], send_out)
+    repeat(0, 1 + count(plane) + count(first), lambda i: drained(both_back.at[0], send_out))
+    repeat(0, 4 - count(own == 0) - count(first), lambda i: drained(both_back.at[0, 0], send_first))
 
 
 def write_out(*refs):
@@ -350,7 +359,7 @@
         scratch_shapes=[pltpu.SMEM((1, 2), jnp.int32)]
         + [pltpu.VMEM(r, bf16) for r in (flat, flat, (Z, Y, C, 2, B), rows, flat, flat)]
         + [pltpu.VMEM((B, B), t) for t in (f32, f32, bf16, bf16, f32, f32, bf16, bf16)]
-        + [dma((6,)), dma((4,)), dma, dma, dma, dma, dma, dma((Z,)), dma((2,)), dma, dma, dma, dma]
+        + [dma((6,)), dma((4,)), dma, dma, dma, dma, dma, dma((Z,)), dma((2,)), dma, dma, dma, dma, dma]
         + [regular((Y,)), regular((Z,)), regular((Z,)), regular],
         compiler_params=pltpu.CompilerParams(
             collective_id=0, has_side_effects=True, vmem_limit_bytes=32 * 1024 * 1024

time: 42.4 us -> 41.5 us (0.979)
  Pallas kernels: 41.6 us -> 40.7 us
    pallas_call x1, Pallas kernels: 40.7 us -> 39.7 us  [shards(): pl.pallas_call(kernel, out_shape=outs, in_specs=[anywhere] * 6, out_specs...]
where the time goes in v10:
time: 41.5 us; the launch traced here: 41.3 us
  Pallas kernels  40.7 us (98%)
  between operations  0.64 us (2%)
    pallas_call x1, Pallas kernels, shards(): pl.pallas_call(kernel, out_shape=outs, in_specs=[anywhere] * 6, out_specs...  39.7 us
    pallas_call x1, Pallas kernels, shards(): pl.pallas_call(write_out, out_shape=outs, in_specs=[pl.BlockSpec(memory_s...  0.96 us

profile of v10, /device:TPU:1, one launch (start us, length us, event | category | flops | bytes accessed | tf_op | source)
XLA Modules:
  0.0 41.3 jit_solution(17647522309120138584)
XLA Ops:
  0.6 39.7 %shard_map.101 = (bf16[8,8,2,2,256]{4,3,2,1,0:T(2,128)(2,1)S(1)}, f32[256,256]{1,0:T(8,128)S(1)}, f32[256,256]{1,0:T(8,128)S(1)}, bf16[256,256]{1,0:T(8,128)(2,1)S(1)}, bf16[256,256]{1,0:T(8,128)(2,1)S(1)}) custom-call(s32[1,2]{1,0:T(1,128)} %refresh_ref.1, bf16[64,2,2,256]{3,2,1,0:T(2,128)(2,1)} %bitcast.12, f32[256,256]{1,0:T(8,128)} %bitcast.10, ...), custom_call_target="tpu_custom_call" | custom-call | tf_op jit(solution)/shard_map/pallas_call | solution.py:354
  40.4 1.0 %shard_map.102 = (bf16[8,8,2,2,256]{4,3,2,1,0:T(2,128)(2,1)}, f32[256,256]{1,0:T(8,128)}, f32[256,256]{1,0:T(8,128)}, bf16[256,256]{1,0:T(8,128)(2,1)}, bf16[256,256]{1,0:T(8,128)(2,1)}) custom-call(bf16[8,8,2,2,256]{4,3,2,1,0:T(2,128)(2,1)S(1)} %get-tuple-element.15.refs_0_, f32[256,256]{1,0:T(8,128)S(1)} %get-tuple-element.16.refs_1_, ...), custom_call_target="tpu_custom_call" | custom-call | tf_op jit(solution)/shard_map/pallas_call | solution.py:368

commit v11 on v10

--- a/solution.py
+++ b/solution.py
@@ -48,9 +48,9 @@
 def kernel(
     refresh_ref, g_ref, ls_ref, rs_ref, lr_ref, rr_ref,
     out_ref, nl_ref, nr_ref, nlr_ref, nrr_ref,
-    refresh, mine, both, relay, block, back, both_back, ls, rs, lr, rr, nl, nr, nlr, nrr,
+    refresh, mine, both, relay, passed, block, back, both_back, ls, rs, lr, rr, nl, nr, nlr, nrr,
     load_sem, store_sem, send_core, recv_core, send_row, send_down, send_up, recv_relay, recv_block,
-    send_back, recv_back, send_first, send_out, recv_out, here_row, here_up, here_proxy, here_corner,
+    send_back, recv_back, send_first, send_out, recv_out, send_passed, recv_passed, here_row, here_up, here_proxy, here_corner,
 ):
     me, own = lax.axis_index("fsdp"), lax.axis_index("own")
     y, z, c = me // (Z * C), (me // C) % Z, me % C
@@ -104,10 +104,12 @@
         signal(barrier, at(y, z, 1 - c))
         repeat(rank + 1, Y, lambda r: signal(barrier, at(ordered(r), z)))
 
+        low = jnp.where(z == Z - 2, y, 0)
+        high = jnp.where(z == Z - 2, y + 1, Y)
+
         @functools.partial(repeat, z + 1, Z)
         def _(pz):
-            for py in range(Y):
-                signal(barrier, at(py, pz))
+            repeat(low, high, lambda py: signal(barrier, at(py, pz)))
 
     @pl.when(others & (z > 0))
     def _():
@@ -134,7 +136,7 @@
             ((refresh_ref, refresh), (ls_ref, ls), (rs_ref, rs), (lr_ref, lr), (rr_ref, rr))
         )
     ]
-    greetings = 1 + rank + Y * z - count(sibling) - count(middle) + count(others & (y == 0)) + Y * count(proxy)
+    greetings = 1 + rank + Y * z - (Y - 1) * last - count(sibling) - count(middle) + count(others & (y == 0)) + Y * count(proxy)
     pl.semaphore_wait(barrier, jnp.where(corner, 2 + rank + Y * (Z - 1), greetings))
 
     def announce():
@@ -187,6 +189,12 @@
 
         @pl.when(z == Z - 1)
         def _():
+            @functools.partial(repeat, y + 1, y + Y)
+            def _(i):
+                py = i & (Y - 1)
+                remote(both.at[py * Z + Z - 2], passed.at[i - y], send_down, recv_passed, at(y, Z - 2))
+
+            down(y, Z - 2)
             for pz in (3, 4, 0):
                 repeat(3, 3 + Y, lambda i, pz=pz: down(i & (Y - 1), pz))
 
@@ -203,7 +211,7 @@
 
         @pl.when(z == Z - 1)
         def _():
-            for pz in (5, 2, 1, 6):
+            for pz in (5, 2, 1):
                 repeat(3, 3 + Y, lambda i, pz=pz: down(i & (Y - 1), pz))
 
         @pl.when(z < Z - 1)
@@ -224,6 +232,17 @@
             def _():
                 pl.semaphore_wait(here_proxy.at[pz], 1)
                 remote(relay.at[pz], block.at[:, z], send_up, recv_block.at[0], at(y, pz, c, 0))
+
+        @pl.when(z == Z - 2)
+        def _():
+            drained(passed.at[1:], recv_passed)
+
+            @functools.partial(repeat, y + 1, y + Y)
+            def _(i):
+                py = i & (Y - 1)
+                remote(passed.at[i - y], block.at[y, Z - 1], send_passed, recv_block.at[1], at(py, Z - 2))
+
+            drained(passed.at[1:], send_passed)
 
         repeat(0, 1 + count(proxy) - count(sibling), lambda i: drained(both.at[:, 0], send_core))
         partners = Y - 1 + (Y - 1) * count(proxy) - count(others & (z == 0))
@@ -357,9 +376,9 @@
         in_specs=[anywhere] * 6,
         out_specs=(anywhere,) * 5,
         scratch_shapes=[pltpu.SMEM((1, 2), jnp.int32)]
-        + [pltpu.VMEM(r, bf16) for r in (flat, flat, (Z, Y, C, 2, B), rows, flat, flat)]
+        + [pltpu.VMEM(r, bf16) for r in (flat, flat, (Z, Y, C, 2, B), (Y, C, 2, B), rows, flat, flat)]
         + [pltpu.VMEM((B, B), t) for t in (f32, f32, bf16, bf16, f32, f32, bf16, bf16)]
-        + [dma((6,)), dma((4,)), dma, dma, dma, dma, dma, dma((Z,)), dma((2,)), dma, dma, dma, dma, dma]
+        + [dma((6,)), dma((4,)), dma, dma, dma, dma, dma, dma((Z,)), dma((2,)), dma, dma, dma, dma, dma, dma, dma]
         + [regular((Y,)), regular((Z,)), regular((Z,)), regular],
         compiler_params=pltpu.CompilerParams(
             collective_id=0, has_side_effects=True, vmem_limit_bytes=32 * 1024 * 1024

time: 41.5 us -> 42.7 us (1.029)
  Pallas kernels: 40.7 us -> 41.8 us
    pallas_call x1, Pallas kernels: 39.7 us -> 40.9 us  [shards(): pl.pallas_call(kernel, out_shape=outs, in_specs=[anywhere] * 6, out_specs...]
where the time goes in v11:
time: 42.7 us; the launch traced here: 42.5 us
  Pallas kernels  41.8 us (98%)
  between operations  0.64 us (1%)
    pallas_call x1, Pallas kernels, shards(): pl.pallas_call(kernel, out_shape=outs, in_specs=[anywhere] * 6, out_specs...  40.9 us
    pallas_call x1, Pallas kernels, shards(): pl.pallas_call(write_out, out_shape=outs, in_specs=[pl.BlockSpec(memory_s...  0.96 us

profile of v11, /device:TPU:1, one launch (start us, length us, event | category | flops | bytes accessed | tf_op | source)
XLA Modules:
  0.0 42.5 jit_solution(17849528699068644110)
XLA Ops:
  0.6 40.9 %shard_map.101 = (bf16[8,8,2,2,256]{4,3,2,1,0:T(2,128)(2,1)S(1)}, f32[256,256]{1,0:T(8,128)S(1)}, f32[256,256]{1,0:T(8,128)S(1)}, bf16[256,256]{1,0:T(8,128)(2,1)S(1)}, bf16[256,256]{1,0:T(8,128)(2,1)S(1)}) custom-call(s32[1,2]{1,0:T(1,128)} %refresh_ref.1, bf16[64,2,2,256]{3,2,1,0:T(2,128)(2,1)} %bitcast.12, f32[256,256]{1,0:T(8,128)} %bitcast.10, ...), custom_call_target="tpu_custom_call" | custom-call | tf_op jit(solution)/shard_map/pallas_call | solution.py:373
  41.5 1.0 %shard_map.102 = (bf16[8,8,2,2,256]{4,3,2,1,0:T(2,128)(2,1)}, f32[256,256]{1,0:T(8,128)}, f32[256,256]{1,0:T(8,128)}, bf16[256,256]{1,0:T(8,128)(2,1)}, bf16[256,256]{1,0:T(8,128)(2,1)}) custom-call(bf16[8,8,2,2,256]{4,3,2,1,0:T(2,128)(2,1)S(1)} %get-tuple-element.15.refs_0_, f32[256,256]{1,0:T(8,128)S(1)} %get-tuple-element.16.refs_1_, ...), custom_call_target="tpu_custom_call" | custom-call | tf_op jit(solution)/shard_map/pallas_call | solution.py:387

commit v12 on v11

--- a/solution.py
+++ b/solution.py
@@ -189,28 +189,28 @@
 
         @pl.when(z == Z - 1)
         def _():
+            for pz in (3, 4, 0):
+                repeat(3, 3 + Y, lambda i, pz=pz: down(i & (Y - 1), pz))
+
+        local(both.at[y * Z + z], block.at[y, z], recv_block.at[last])
+
+        @functools.partial(repeat, z + 1, Z)
+        def _(pz):
+            local(both.at[y * Z + pz], relay.at[pz, y], recv_relay.at[pz])
+
+        @functools.partial(repeat, rank + 1, Y - count(others & (z == 0)))
+        def _(r):
+            pl.semaphore_wait(here_row.at[r], 1)
+            to_row(ordered(r))
+
+        @pl.when(z == Z - 1)
+        def _():
             @functools.partial(repeat, y + 1, y + Y)
             def _(i):
                 py = i & (Y - 1)
                 remote(both.at[py * Z + Z - 2], passed.at[i - y], send_down, recv_passed, at(y, Z - 2))
 
             down(y, Z - 2)
-            for pz in (3, 4, 0):
-                repeat(3, 3 + Y, lambda i, pz=pz: down(i & (Y - 1), pz))
-
-        local(both.at[y * Z + z], block.at[y, z], recv_block.at[last])
-
-        @functools.partial(repeat, z + 1, Z)
-        def _(pz):
-            local(both.at[y * Z + pz], relay.at[pz, y], recv_relay.at[pz])
-
-        @functools.partial(repeat, rank + 1, Y - count(others & (z == 0)))
-        def _(r):
-            pl.semaphore_wait(here_row.at[r], 1)
-            to_row(ordered(r))
-
-        @pl.when(z == Z - 1)
-        def _():
             for pz in (5, 2, 1):
                 repeat(3, 3 + Y, lambda i, pz=pz: down(i & (Y - 1), pz))
 

time: 42.7 us -> 42.7 us (level)
  no operation moved by 1% of the time
where the time goes in v12:
time: 42.7 us; the launch traced here: 42.5 us
  Pallas kernels  41.9 us (98%)
  between operations  0.64 us (1%)
    pallas_call x1, Pallas kernels, shards(): pl.pallas_call(kernel, out_shape=outs, in_specs=[anywhere] * 6, out_specs...  40.9 us
    pallas_call x1, Pallas kernels, shards(): pl.pallas_call(write_out, out_shape=outs, in_specs=[pl.BlockSpec(memory_s...  0.96 us

profile of v12, /device:TPU:1, one launch (start us, length us, event | category | flops | bytes accessed | tf_op | source)
XLA Modules:
  0.0 42.5 jit_solution(16493339490641604725)
XLA Ops:
  0.6 40.9 %shard_map.101 = (bf16[8,8,2,2,256]{4,3,2,1,0:T(2,128)(2,1)S(1)}, f32[256,256]{1,0:T(8,128)S(1)}, f32[256,256]{1,0:T(8,128)S(1)}, bf16[256,256]{1,0:T(8,128)(2,1)S(1)}, bf16[256,256]{1,0:T(8,128)(2,1)S(1)}) custom-call(s32[1,2]{1,0:T(1,128)} %refresh_ref.1, bf16[64,2,2,256]{3,2,1,0:T(2,128)(2,1)} %bitcast.12, f32[256,256]{1,0:T(8,128)} %bitcast.10, ...), custom_call_target="tpu_custom_call" | custom-call | tf_op jit(solution)/shard_map/pallas_call | solution.py:373
  41.5 1.0 %shard_map.102 = (bf16[8,8,2,2,256]{4,3,2,1,0:T(2,128)(2,1)}, f32[256,256]{1,0:T(8,128)}, f32[256,256]{1,0:T(8,128)}, bf16[256,256]{1,0:T(8,128)(2,1)}, bf16[256,256]{1,0:T(8,128)(2,1)}) custom-call(bf16[8,8,2,2,256]{4,3,2,1,0:T(2,128)(2,1)S(1)} %get-tuple-element.15.refs_0_, f32[256,256]{1,0:T(8,128)S(1)} %get-tuple-element.16.refs_1_, ...), custom_call_target="tpu_custom_call" | custom-call | tf_op jit(solution)/shard_map/pallas_call | solution.py:387
